TPU v7x, 32 devices: a whole 2x2x4 slice. The times are simulated.
32 devices in a mesh: groups: 2 (over x), ctx: 16 (over z, y, core).
Axes of the slice: x: 2, y: 2, z: 4, core: 2. Of those that a mesh axis runs over, the one named last changes fastest.
Arguments:
- tokens: bfloat16 [4096, 2880], P(('groups', 'ctx')), parts along dimension 0, may hold values from -6 to 6
- lengths: int32 [8], P('groups'), parts along dimension 0, may hold values from 1 to 1536, 2048 in all
- attn_gain: float32 [2880], replicated, may hold values from 0.1 to 1.9
- w_query: bfloat16 [2880, 2048], P('ctx'), may hold values from -2 to 2
- w_key: bfloat16 [2880, 256], replicated, may hold values from -1 to 1
- w_value: bfloat16 [2880, 256], replicated, may hold values from -0.109375 to 0.109375
- sinks: float32 [32], replicated, may hold values from -2 to 4
- w_out: bfloat16 [2048, 2880], P('ctx'), may hold values from -0.5 to 0.5
- moe_gain: float32 [2880], replicated, may hold values from 0.1 to 1.9
- routes: int32 [4096, 4], P(('groups', 'ctx')), parts along dimension 0, may hold values from 0 to 7, all different within a row; in each aligned block of 128 rows (0 to 127, 128 to 255, ...) at most 68 rows name the same one
- route_weights: float32 [4096, 4], P(('groups', 'ctx')), parts along dimension 0, may hold values from 0.05 to 1
- w_gate: bfloat16 [16, 2880, 768], P('ctx'), may hold values from -0.109375 to 0.109375
- w_up: bfloat16 [16, 2880, 768], P('ctx'), may hold values from -0.109375 to 0.109375
- w_down: bfloat16 [16, 768, 2880], P('ctx'), may hold values from -0.15625 to 0.15625
Outputs:
- result: bfloat16 [4096, 2880], P(('groups', 'ctx')), parts along dimension 0
There are 2 independent parts, one for each index of `groups`. A program takes and returns all parts, laid end to end along the dimension named above; an argument that names none is the same for every part. Nothing has to cross between parts.
Inputs may be any that keep to these rules, and one draw needn't show every extreme that they name: lengths of the 4 requests packed in order into the 2048 tokens; they sum to 2048. `routes`: each token names 4 different experts; among the 128 tokens of one index of ctx no expert is named by more than 68 tokens, a bound that some block reaches.
All inputs are finite; a program needn't handle non-finite values.
Results may differ from a plain program's by a relative error of at most 0.014.
Values may be sent and summed in bfloat16 or wider, within the bound.
No kernel may reach another device: no remote copies, remote signals or barrier semaphores. Data moves between devices by JAX's collectives and lax.ppermute only.
A program may use at most 128 MiB of HBM per device.

v0:
```python
import jax
import jax.numpy as jnp
import numpy as np
from jax import lax
from jax.experimental import pallas as pl
from jax.experimental.pallas import tpu as pltpu
from jax.sharding import PartitionSpec as P

HD = 64
SPLITS = 2
TOP = 4
PLANE = 4
ORDER = (0, 2, 1, 3)

EPS = 1e-05
THETA = 150000.0
ALPHA = 1.702
SCALE = 0.125
NEGATIVE = -1e30


def swap_with(x, axis, bits):
    return lax.ppermute(x, axis, [(i, i ^ bits) for i in range(lax.axis_size(axis))])


def after(value, *earlier):
    return lax.optimization_barrier((value, *earlier))[0]


def gate(value, *earlier):
    anywhere = pl.BlockSpec(memory_space=pl.ANY)
    return pl.pallas_call(
        lambda *refs: None,
        out_shape=jax.ShapeDtypeStruct(value.shape, value.dtype),
        in_specs=[anywhere] * (1 + len(earlier)),
        out_specs=anywhere,
        input_output_aliases={0: 0},
        compiler_params=pltpu.CompilerParams(vmem_limit_bytes=60 * 1024 * 1024),
    )(value, *earlier)


def forwarded(held, planes, hops):
    return {
        k: swap_with(held[k & (k - 1)], "ctx", PLANE * (k & -k))
        for k in range(planes - 1, 0, -1)
        if k.bit_count() == hops and k not in held
    }


def over_planes(block, planes):
    held = {0: block}
    for hops in range(1, planes.bit_length()):
        held.update(forwarded(held, planes, hops))
    return held


def together(*values):
    flat, tree = jax.tree.flatten(values)
    anywhere = pl.BlockSpec(memory_space=pl.ANY)
    out = pl.pallas_call(
        lambda *refs: None,
        out_shape=[jax.ShapeDtypeStruct(x.shape, x.dtype) for x in flat],
        in_specs=[anywhere] * len(flat),
        out_specs=[anywhere] * len(flat),
        input_output_aliases={i: i for i in range(len(flat))},
        compiler_params=pltpu.CompilerParams(vmem_limit_bytes=60 * 1024 * 1024),
    )(*flat)
    return jax.tree.unflatten(tree, out)


def lane_padded(width):
    return -(-width // 128) * 128


def rms_scale(values, gain_vec):
    wide = values.astype(jnp.float32)
    inverse = lax.rsqrt(jnp.mean(wide * wide, axis=-1, keepdims=True) + EPS)
    return (wide * inverse * gain_vec).astype(jnp.bfloat16)


def angle_tables(positions):
    half_size = HD // 2
    freqs = np.tile(THETA ** (-np.arange(half_size) / half_size), 4).astype(np.float32)
    sign = np.tile(np.repeat(np.array([-1.0, 1.0], np.float32), half_size), 2)
    angles = positions.astype(jnp.float32)[:, None] * freqs[None, :]
    return jnp.cos(angles), jnp.sin(angles) * sign[None, :]


def turn(tile, first, cosine, sine):
    width = 2 * HD
    other = jnp.where(first, pltpu.roll(tile, width - HD // 2, 1), pltpu.roll(tile, HD // 2, 1))
    return tile * cosine + other * sine


def whole_call(body, out_shapes, operands, scalars=1, scratch=(), limit=24, flops=0, waits=0):
    anywhere = pl.BlockSpec(memory_space=pl.ANY)
    smem = pl.BlockSpec(memory_space=pltpu.SMEM)
    vmem = pl.BlockSpec(memory_space=pltpu.VMEM)
    size = sum(x.size * x.dtype.itemsize for x in operands)
    return pl.pallas_call(
        body,
        out_shape=out_shapes,
        in_specs=[smem] * scalars + [vmem] * (len(operands) - scalars - waits) + [anywhere] * waits,
        out_specs=jax.tree.map(lambda _: vmem, out_shapes),
        scratch_shapes=list(scratch),
        compiler_params=pltpu.CompilerParams(vmem_limit_bytes=limit * 1024 * 1024),
        cost_estimate=pl.CostEstimate(flops=flops, bytes_accessed=size, transcendentals=0),
    )(*operands)


def split_query(info, w_query, planes):
    rows = w_query.shape[0]
    cols = w_query.shape[1] // (planes * PLANE)
    if cols % 128:
        in_plane = info[0] % PLANE
        parts = jnp.stack(
            [
                jnp.concatenate(
                    [
                        w_query[:, (PLANE * zz + j) * cols:(PLANE * zz + j + 1) * cols]
                        for zz in range(planes)
                    ],
                    axis=1,
                )
                for j in range(PLANE)
            ]
        )
        return [
            lax.dynamic_index_in_dim(parts, in_plane ^ m, 0, keepdims=False) for m in range(PLANE)
        ]

    def body(info_ref, w_ref, *outs):
        in_plane = info_ref[0] % PLANE
        for m in range(PLANE):
            for zz in range(planes):
                start = pl.multiple_of((PLANE * zz + (in_plane ^ m)) * cols, 128)
                outs[m][:, zz * cols:(zz + 1) * cols] = w_ref[:, pl.ds(start, cols)]

    shape = jax.ShapeDtypeStruct((rows, planes * cols), jnp.bfloat16)
    return whole_call(body, [shape] * PLANE, (info, w_query))


def prepare(tokens, gain, w_key, w_value, routes, route_weights, cosine, sine, earlier):
    rows, width = tokens.shape
    padded = lane_padded(width)
    key_cols = w_key.shape[1]

    def body(tok_ref, gain_ref, key_ref, val_ref, route_ref, weight_ref, cos_ref, sin_ref, _,
             rows_ref, normed_ref, kv_ref, wide):
        for start in range(0, width, 128):
            size = min(128, width - start)
            piece = tok_ref[start:start + size, :].astype(jnp.float32)
            if size < 128:
                piece = jnp.concatenate([piece, jnp.zeros((128 - size, rows), jnp.float32)], axis=0)
            wide[:, start:start + 128] = piece.T
        values = wide[...]
        rows_ref[...] = values.astype(jnp.bfloat16)
        mean = jnp.sum(values * values, axis=1, keepdims=True) / width
        normed_ref[...] = (values * lax.rsqrt(mean + EPS) * gain_ref[...]).astype(jnp.bfloat16)
        normed = normed_ref[:, :width]
        raw_key = jnp.dot(normed, key_ref[...], preferred_element_type=jnp.float32)
        lane = lax.broadcasted_iota(jnp.int32, (rows, 2 * HD), 1)
        first = lane % HD < HD // 2
        for start in range(0, key_cols, 2 * HD):
            lanes = slice(start, start + 2 * HD)
            kv_ref[:, lanes] = turn(raw_key[:, lanes], first, cos_ref[...], sin_ref[...]).astype(
                jnp.bfloat16
            )
        kv_ref[:, key_cols:2 * key_cols] = jnp.dot(
            normed, val_ref[...], preferred_element_type=jnp.float32
        ).astype(jnp.bfloat16)
        left = weight_ref[...]
        facts = [route_ref[...].astype(jnp.float32)]
        for _ in range(3):
            part = left.astype(jnp.bfloat16).astype(jnp.float32)
            facts.append(part)
            left = left - part
        facts.append(jnp.zeros((128 - 4 * TOP, rows), jnp.float32))
        kv_ref[:, 2 * key_cols:] = jnp.concatenate(facts, axis=0).T.astype(jnp.bfloat16)

    gain = jnp.pad(gain, (0, padded - width))[None]
    return whole_call(
        body,
        [
            jax.ShapeDtypeStruct((rows, padded), jnp.bfloat16),
            jax.ShapeDtypeStruct((rows, padded), jnp.bfloat16),
            jax.ShapeDtypeStruct((rows, 2 * key_cols + 128), jnp.bfloat16),
        ],
        (tokens.T, gain, w_key, w_value, routes.T, route_weights.T, cosine, sine, earlier),
        scalars=0,
        waits=1,
        scratch=[pltpu.VMEM((rows, padded), jnp.float32)],
        flops=1_000_000_000,
    )


def cut_pairs(two, c_two, pairs, cols):
    rows = two.shape[0]

    def body(two_ref, c_ref, out_ref):
        for b in range(pairs):
            lanes = slice(b * cols, (b + 1) * cols)
            out_ref[b, :rows, :] = two_ref[:, lanes]
            out_ref[b, rows:, :] = c_ref[:, lanes]

    return whole_call(
        body, jax.ShapeDtypeStruct((pairs, 2 * rows, cols), jnp.bfloat16), (two, c_two), scalars=0
    )


def joined(*blocks):
    rows = [block.shape[0] for block in blocks]

    def body(*refs):
        start = 0
        for ref, count in zip(refs[:-1], rows):
            refs[-1][start:start + count] = ref[...]
            start += count

    out = jax.ShapeDtypeStruct((sum(rows),) + blocks[0].shape[1:], blocks[0].dtype)
    return whole_call(body, out, blocks, scalars=0)


def half_rows(info, weight, earlier):
    rows, width = weight.shape
    padded = lane_padded(width)

    def body(info_ref, weight_ref, _, out_ref):
        at = pl.multiple_of(info_ref[1] * (rows // 2), rows // 2)
        out_ref[:, :width] = weight_ref[pl.ds(at, rows // 2), :]
        out_ref[:, width:] = jnp.zeros((rows // 2, padded - width), jnp.bfloat16)

    vmem = pl.BlockSpec(memory_space=pltpu.VMEM)
    return pl.pallas_call(
        body,
        out_shape=jax.ShapeDtypeStruct((rows // 2, padded), jnp.bfloat16),
        in_specs=[pl.BlockSpec(memory_space=pltpu.SMEM), vmem, pl.BlockSpec(memory_space=pl.ANY)],
        out_specs=vmem,
    )(info, weight, earlier)


def own_half(info, pieces, normed, earlier):
    rows, cols = pieces[0].shape

    def body(info_ref, p0, p1, p2, p3, normed_ref, *rest):
        mine_ref, rest_ref, again_ref = rest[-3:]
        odd = info_ref[0] % 2 == 1
        half = info_ref[1]
        again_ref[...] = normed_ref[...]
        for swapped in range(2):
            @pl.when(odd if swapped else jnp.logical_not(odd))
            def _():
                near = (p1, p0) if swapped else (p0, p1)
                far = (p3, p2) if swapped else (p2, p3)
                near = jnp.concatenate([near[0][...], near[1][...]], axis=0)
                far = jnp.concatenate([far[0][...], far[1][...]], axis=0)

                @pl.when(half == 0)
                def _():
                    mine_ref[...] = near
                    rest_ref[...] = far

                @pl.when(half == 1)
                def _():
                    mine_ref[...] = far
                    rest_ref[...] = near

    shape = jax.ShapeDtypeStruct((2 * rows, cols), jnp.bfloat16)
    again = jax.ShapeDtypeStruct(normed.shape, normed.dtype)
    return whole_call(
        body, [shape, shape, again], (info, *pieces, normed, *earlier), waits=len(earlier)
    )


def query_kernel(planes, kv_heads, rows_of, info, nb_ref, cos_ref, sin_ref, *rest):
    pieces = rest[: 2 * planes]
    q_ref, weights, sem = rest[2 * planes:]
    copies = [
        pltpu.make_async_copy(piece, weights.at[i], sem.at[i]) for i, piece in enumerate(pieces)
    ]
    for copy in copies:
        copy.start()
    me, half = info[0], info[1]
    width = 2 * HD
    wide = 2 * rows_of
    lane = lax.broadcasted_iota(jnp.int32, (wide, width), 1)
    low_half = lane < HD
    first = lane % HD < HD // 2
    for r in range(2):
        total = None
        for k in range(planes):
            for side in range(2):
                chosen = half if side == 0 else 1 - half
                pair = (me ^ (PLANE * k + 2 * chosen)) // 2
                if r == 0:
                    copies[2 * k + side].wait()
                term = jnp.dot(
                    nb_ref[pair, r * wide:(r + 1) * wide, :], weights[2 * k + side],
                    preferred_element_type=jnp.float32,
                )
                total = term if total is None else total + term
        at = slice(r * wide, (r + 1) * wide)
        for g in range(kv_heads):
            tile = total[:, g * width:(g + 1) * width]
            tile = turn(tile, first, cos_ref[at, :], sin_ref[at, :]) * SCALE
            moved = pltpu.roll(tile, HD, 1)
            if g % 2 == 0:
                heads = (jnp.where(low_half, tile, 0.0), jnp.where(low_half, moved, 0.0))
            else:
                heads = (jnp.where(low_half, 0.0, moved), jnp.where(low_half, 0.0, tile))
            for u in range(2):
                for m in range(2):
                    start = (2 * (2 * r + m) + u) * rows_of
                    q_ref[g, start:start + rows_of, :] = heads[u][
                        m * rows_of:(m + 1) * rows_of
                    ].astype(jnp.bfloat16)


def make_queries(info, nb, cosine, sine, weights, planes, cols):
    rows = cosine.shape[0]
    kv_heads = planes * cols // (2 * HD)

    def body(*refs):
        query_kernel(planes, kv_heads, rows // PLANE, *refs)

    smem = pl.BlockSpec(memory_space=pltpu.SMEM)
    vmem = pl.BlockSpec(memory_space=pltpu.VMEM)
    anywhere = pl.BlockSpec(memory_space=pl.ANY)
    return pl.pallas_call(
        body,
        out_shape=jax.ShapeDtypeStruct((kv_heads, 2 * rows, 2 * HD), jnp.bfloat16),
        in_specs=[smem] + [vmem] * 3 + [anywhere] * len(weights),
        out_specs=vmem,
        scratch_shapes=[
            pltpu.VMEM((len(weights),) + weights[0].shape, jnp.bfloat16),
            pltpu.SemaphoreType.DMA((len(weights),)),
        ],
        compiler_params=pltpu.CompilerParams(vmem_limit_bytes=56 * 1024 * 1024),
        cost_estimate=pl.CostEstimate(
            flops=8_000_000_000, bytes_accessed=8_000_000, transcendentals=0
        ),
    )(info, nb, cosine, sine, *weights)


def attention_kernel(planes, kv_heads, rows_of, info, lo_first, sink_ref, q_ref, lo_ref, pos_ref,
                     own_kv, y_kv, c_kv, cy_kv, out_ref, bias_ref, score_ref, max_ref, acc_ref):
    me = info[0]
    plane = me // PLANE
    rows = PLANE * rows_of
    width = 2 * HD
    wide = 2 * rows_of
    cols = out_ref.shape[2]
    earliest = lo_first[0]
    for m in range(1, PLANE):
        earliest = jnp.minimum(earliest, lo_first[m])

    def for_needed(act):
        def step(k, carry):
            other = plane ^ k

            @pl.when((other <= plane) & (earliest < (other + 1) * rows))
            def _():
                act(k)

            return carry

        lax.fori_loop(0, planes, step, 0)

    def chunk(k, lanes):
        at = pl.ds(pl.multiple_of(k * rows_of, rows_of), rows_of)
        return jnp.concatenate(
            [own_kv[at, lanes], y_kv[at, lanes], c_kv[at, lanes], cy_kv[at, lanes]], axis=0
        )

    key_iota = lax.broadcasted_iota(jnp.int32, (1, rows_of), 1)

    def set_bias(k):
        key_pos = jnp.concatenate(
            [(me ^ (PLANE * k + m)) * rows_of + key_iota for m in ORDER], axis=1
        )
        allowed = (key_pos >= lo_ref[...]) & (key_pos <= pos_ref[...])
        bias_ref[k] = jnp.where(allowed, 0.0, NEGATIVE)

    for_needed(set_bias)

    lane_q = lax.broadcasted_iota(jnp.int32, (wide, width), 1) < HD
    lane_k = lax.broadcasted_iota(jnp.int32, (rows, width), 1) < HD
    row_q = lax.broadcasted_iota(jnp.int32, (wide, width), 0) < rows_of

    def two_heads(pair, carry):
        key_lanes = pl.ds(pl.multiple_of(pair * width, width), width)
        val_lanes = pl.ds(pl.multiple_of((kv_heads // 2 + pair) * width, width), width)
        sinks = [
            jnp.where(row_q, sink_ref[4 * pair + 2 * i], sink_ref[4 * pair + 2 * i + 1])
            for i in range(2)
        ]
        for i in range(2):
            for m in range(PLANE):
                max_ref[i, m * wide:(m + 1) * wide, :] = sinks[i]

        def scores(k):
            keys = chunk(k, key_lanes)
            for m in range(PLANE):
                at = slice(m * wide, (m + 1) * wide)
                bias = bias_ref[k, m * rows_of:(m + 1) * rows_of, :]
                for i in range(2):
                    score = lax.dot_general(
                        q_ref[2 * pair + i, at, :], keys, (((1,), (1,)), ((), ())),
                        preferred_element_type=jnp.float32,
                    )
                    score = (score.reshape(2, rows_of, rows) + bias[None]).reshape(wide, rows)
                    score_ref[i, k, at, :] = score
                    top = max_ref[i, at, :]
                    for start in range(0, rows, width):
                        top = jnp.maximum(top, score[:, start:start + width])
                    max_ref[i, at, :] = top

        for_needed(scores)

        for i in range(2):
            mine = lane_q if i == 0 else ~lane_q
            for m in range(PLANE):
                at = slice(m * wide, (m + 1) * wide)
                top = jnp.max(max_ref[i, at, :], axis=1, keepdims=True)
                top = jnp.broadcast_to(top, (wide, width))
                max_ref[i, at, :] = top
                acc_ref[i, at, :] = jnp.where(mine, 0.0, jnp.exp(sinks[i] - top))

        def gather(k):
            values = chunk(k, val_lanes)
            for i in range(2):
                mine_k = lane_k if i == 0 else ~lane_k
                vals = jnp.where(mine_k, values, jnp.bfloat16(1.0))
                for m in range(PLANE):
                    at = slice(m * wide, (m + 1) * wide)
                    top = max_ref[i, at, :]
                    probs = jnp.concatenate(
                        [
                            jnp.exp(score_ref[i, k, at, start:start + width] - top).astype(
                                jnp.bfloat16
                            )
                            for start in range(0, rows, width)
                        ],
                        axis=1,
                    )
                    acc_ref[i, at, :] += jnp.dot(probs, vals, preferred_element_type=jnp.float32)

        for_needed(gather)

        for i in range(2):
            g = 2 * pair + i
            for m in range(PLANE):
                acc = acc_ref[i, m * wide:(m + 1) * wide, :]
                done = acc / pltpu.roll(acc, HD, 1)
                one, two = done[:rows_of], done[rows_of:]
                low = lane_q[:rows_of]
                if i == 0:
                    both = jnp.where(low, one, pltpu.roll(two, HD, 1))
                else:
                    both = jnp.where(low, pltpu.roll(one, HD, 1), two)
                both = both.astype(jnp.bfloat16)
                for j in range(width // cols):
                    out_ref[g * (width // cols) + j, m * rows_of:(m + 1) * rows_of, :] = both[
                        :, j * cols:(j + 1) * cols
                    ]
        return carry

    lax.fori_loop(0, kv_heads // 2, two_heads, 0)


def attend(info, lo_first, sinks, queries, lo, pos, kv, planes, cols):
    rows = pos.shape[0]
    kv_heads = queries.shape[0]

    def body(*refs):
        attention_kernel(planes, kv_heads, rows // PLANE, *refs)

    return whole_call(
        body,
        jax.ShapeDtypeStruct((planes, rows, cols), jnp.bfloat16),
        (info, lo_first, sinks, queries, lo, pos, *kv),
        scalars=3,
        scratch=[
            pltpu.VMEM((planes, rows, rows), jnp.float32),
            pltpu.VMEM((2, planes, 2 * rows, rows), jnp.float32),
            pltpu.VMEM((2, 2 * rows, 2 * HD), jnp.float32),
            pltpu.VMEM((2, 2 * rows, 2 * HD), jnp.float32),
        ],
        limit=58,
        flops=16_000_000_000,
    )


def project(info, attended, own, mine, twin, places):
    planes, rows, cols = attended.shape
    width = own.shape[1]
    padded = lane_padded(width)
    wide = rows // 2

    def body(info_ref, att_ref, own_ref, *rest):
        send_ref, keep_ref, att, weight = rest[2 * len(places):]
        plane, half = info_ref[0] // PLANE, info_ref[1]
        short = cols // 2
        weight[:cols, :] = own_ref[...]
        for k in range(planes):
            att[:, k * cols:(k + 1) * cols] = att_ref[plane ^ k]
        for i, ks in enumerate(places):
            for side in range(2):
                chosen = half if side == 0 else 1 - half
                for j, k in enumerate(ks):
                    at = pl.multiple_of(k * cols + chosen * short, short)
                    weight[pl.ds(at, short), :] = rest[side * len(places) + i][
                        j * short:(j + 1) * short, :width
                    ]
        for start in range(0, width, 640):
            lanes = slice(start, min(width, start + 640))
            send_ref[:, lanes] = jnp.dot(
                att[wide:], weight[:, lanes], preferred_element_type=jnp.float32
            ).astype(jnp.bfloat16)
            keep_ref[:, lanes] = jnp.dot(
                att[:wide], weight[:, lanes], preferred_element_type=jnp.float32
            )
        send_ref[:, width:] = jnp.zeros((wide, padded - width), jnp.bfloat16)
        keep_ref[:, width:] = jnp.zeros((wide, padded - width), jnp.float32)

    return whole_call(
        body,
        [
            jax.ShapeDtypeStruct((wide, padded), jnp.bfloat16),
            jax.ShapeDtypeStruct((wide, padded), jnp.float32),
        ],
        (info, attended, own, *mine, *twin),
        scratch=[
            pltpu.VMEM((rows, planes * cols), jnp.bfloat16),
            pltpu.VMEM((planes * cols, width), jnp.bfloat16),
        ],
        flops=4_000_000_000,
    )


def add_core(keep, got):
    rows, width = keep.shape[0] // 2, keep.shape[1]

    def body(keep_ref, got_ref, send_ref, rest_ref):
        rest_ref[...] = keep_ref[:rows] + got_ref[:rows].astype(jnp.float32)
        send_ref[...] = (keep_ref[rows:] + got_ref[rows:].astype(jnp.float32)).astype(jnp.bfloat16)

    return whole_call(
        body,
        [
            jax.ShapeDtypeStruct((rows, width), jnp.bfloat16),
            jax.ShapeDtypeStruct((rows, width), jnp.float32),
        ],
        (keep, got),
        scalars=0,
    )


def mix(tokens, keep, got, gain):
    rows, padded = tokens.shape
    width = gain.shape[0]

    def body(tokens_ref, keep_ref, got_ref, gain_ref, mixed_ref, in_ref):
        mixed = (
            tokens_ref[...].astype(jnp.float32) + keep_ref[...] + got_ref[...].astype(jnp.float32)
        ).astype(jnp.bfloat16)
        mixed_ref[...] = mixed
        values = mixed.astype(jnp.float32)
        mean = jnp.sum(values * values, axis=1, keepdims=True) / width
        in_ref[...] = (values * lax.rsqrt(mean + EPS) * gain_ref[...]).astype(jnp.bfloat16)

    shape = jax.ShapeDtypeStruct((rows, padded), jnp.bfloat16)
    gain = jnp.pad(gain, (0, padded - width))[None]
    return whole_call(body, [shape, shape], (tokens, keep, got, gain), scalars=0)


def finish(width, mixed, total, *got):
    rows = mixed.shape[0]

    def body(mixed_ref, total_ref, *rest):
        out_ref = rest[-1]
        for start in range(0, width, 128):
            size = min(128, width - start)
            lanes = slice(start, start + size)
            value = mixed_ref[:, lanes].astype(jnp.float32) + total_ref[:, lanes]
            for ref in rest[:-1]:
                value += ref[:, lanes].astype(jnp.float32)
            if size < 128:
                value = jnp.concatenate([value, jnp.zeros((rows, 128 - size), jnp.float32)], axis=1)
            out_ref[lanes, :] = value.T[:size].astype(jnp.bfloat16)

    out = jax.ShapeDtypeStruct((width, rows), jnp.bfloat16)
    return whole_call(body, out, (mixed, total, *got), scalars=0).T


def by_columns(hidden, down):
    return lax.dot_general(hidden, down, (((1,), (1,)), ((), ())), preferred_element_type=jnp.float32)


def expert(x, row_weights, slabs):
    rows, padded = x.shape
    width, hidden = slabs[0].shape[1:]

    def body(x_ref, row_ref, gate_ref, up_ref, down_ref, out_ref, held, sem):
        copies = [
            pltpu.make_async_copy(ref.at[side], held.at[3 * side + i], sem.at[3 * side + i])
            for side in range(2)
            for i, ref in enumerate((gate_ref, up_ref, down_ref))
        ]
        for copy in copies[:2]:
            copy.start()
        total = None
        for side in range(2):
            i = 3 * side
            inputs = x_ref[:, :width]
            copies[i].wait()
            copies[i + 2].start()
            gate_val = jnp.dot(inputs, held[i], preferred_element_type=jnp.float32)
            copies[i + 1].wait()
            if side == 0:
                copies[3].start()
                copies[4].start()
            up_val = jnp.dot(inputs, held[i + 1], preferred_element_type=jnp.float32)
            rows_in = ((up_val + 1.0) * gate_val * jax.nn.sigmoid(ALPHA * gate_val)).astype(
                jnp.bfloat16
            )
            copies[i + 2].wait()
            term = by_columns(rows_in, held[i + 2])
            total = term if total is None else total + term
        out_ref[:, :width] = (total * row_ref[...]).astype(jnp.bfloat16)
        out_ref[:, width:] = jnp.zeros((rows, padded - width), jnp.bfloat16)

    vmem = pl.BlockSpec(memory_space=pltpu.VMEM)
    return pl.pallas_call(
        body,
        out_shape=jax.ShapeDtypeStruct((rows, padded), jnp.bfloat16),
        in_specs=[vmem, vmem] + [pl.BlockSpec(memory_space=pl.ANY)] * 3,
        out_specs=vmem,
        scratch_shapes=[
            pltpu.VMEM((6, width, hidden), jnp.bfloat16),
            pltpu.SemaphoreType.DMA((6,)),
        ],
        compiler_params=pltpu.CompilerParams(vmem_limit_bytes=48 * 1024 * 1024),
        cost_estimate=pl.CostEstimate(
            flops=12 * rows * width * hidden,
            bytes_accessed=12 * width * hidden,
            transcendentals=2 * rows * hidden,
        ),
    )(x, row_weights, *slabs)


def per_device(
    tokens,
    lengths,
    attn_gain,
    w_query,
    w_key,
    w_value,
    sinks,
    w_out,
    moe_gain,
    routes,
    route_weights,
    w_gate,
    w_up,
    w_down,
):
    tok_rows, model_width = tokens.shape
    devices = lax.axis_size("ctx")
    planes = devices // PLANE
    me = lax.axis_index("ctx")
    in_plane = me % PLANE
    half = lax.axis_index("groups") % 2
    info = jnp.stack([me, half]).astype(jnp.int32)
    cols = w_query.shape[1] // devices
    q_rows = w_query.shape[0]

    cores = [[i, i + 1] for i in range(0, devices, 2)]
    slabs = [
        lax.all_gather(w, "ctx", axis=0, tiled=True, axis_index_groups=cores)
        for w in (w_gate, w_up, jnp.swapaxes(w_down, 1, 2))
    ]

    parts = split_query(info, w_query, planes)
    got = [swap_with(parts[m], "ctx", m) for m in (1, 2, 3)]

    span = jnp.arange(tok_rows, dtype=jnp.int32)
    positions = jnp.concatenate([(me ^ m) * tok_rows + span for m in ORDER])
    cosine, sine = angle_tables(positions)
    tokens, normed, kv = prepare(
        tokens, attn_gain, w_key, w_value, routes, route_weights, cosine[:tok_rows], sine[:tok_rows],
        parts[1],
    )
    kv_width, fact_width = w_key.shape[1] + w_value.shape[1], 4 * TOP

    w_mine, w_rest, late_normed = own_half(info, [parts[0], *got], normed, [])
    w_of = {0: w_mine}
    w_of.update(forwarded(w_of, planes, 1))
    kv_of = {0: kv}
    kv_of.update(forwarded(kv_of, planes, 1))
    y_normed = swap_with(late_normed, "ctx", 2)
    w_of, kv_of, y_normed = together(w_of, kv_of, y_normed)

    w_twin = {k: swap_with(w_of[k], "groups", 1) for k in w_of if k}
    w_of.update(forwarded(w_of, planes, 2))
    for hops in range(2, planes.bit_length()):
        kv_of.update(forwarded(kv_of, planes, hops))
    across = planes // 2
    wo_half = half_rows(info, w_out, y_normed)
    wo_of = {across: swap_with(wo_half, "ctx", PLANE * across)}
    w_of, w_twin, kv_of, y_normed, wo_half, wo_of = together(
        w_of, w_twin, kv_of, y_normed, wo_half, wo_of
    )

    for hops in range(3, planes.bit_length()):
        w_of.update(forwarded(w_of, planes, hops))
    two = joined(normed, y_normed)
    nb = cut_pairs(two, swap_with(two, "ctx", 1), devices // 2, 2 * q_rows)
    for k in w_of:
        if k and k not in w_twin:
            w_of[k] = gate(w_of[k], nb)
            w_twin[k] = swap_with(w_of[k], "groups", 1)
    own_kv = joined(*[kv_of[k] for k in range(planes)])
    y_kv = swap_with(own_kv, "ctx", 2)
    wo_twin = [swap_with(wo_of[across], "groups", 1)]
    wo_got, wo_ks, known = [wo_of[across]], [[across]], [0, across]
    bit = across // 2
    while bit:
        wo_got.append(swap_with(joined(wo_half, *wo_got), "ctx", PLANE * bit))
        wo_ks.append([k ^ bit for k in known])
        known += wo_ks[-1]
        bit //= 2
    w_twin, own_kv, y_kv, wo_got, wo_twin = together(w_twin, own_kv, y_kv, wo_got, wo_twin)

    c_kv = swap_with(own_kv, "ctx", 1)
    cy_kv = swap_with(y_kv, "ctx", 1)
    q_weights = [w_of[0], w_rest]
    for k in range(1, planes):
        q_weights += [w_of[k], w_twin[k]]
    wo_twin += [swap_with(rows, "groups", 1) for rows in wo_got[1:]]

    experts_num = devices // SPLITS
    capacity = tok_rows * TOP * 17 // (16 * experts_num)
    padded = -(-capacity // 8) * 8

    def facts_of(block):
        return block[:, kv_width:kv_width + fact_width].reshape(planes, tok_rows, fact_width).astype(
            jnp.float32
        )

    own_facts, far_facts = facts_of(own_kv), facts_of(y_kv)
    mine_expert = (me // SPLITS).astype(jnp.float32)
    other_expert = ((me // SPLITS) ^ 1).astype(jnp.float32)
    earlier = (span[:, None] < span[None, :]).astype(jnp.bfloat16)
    slot_ids = jnp.arange(padded, dtype=jnp.float32)

    def chosen_rows(known, expert_id):
        match = known[:, :, :TOP] == expert_id
        hit = jnp.any(match, axis=2)
        weight = sum(known[:, :, i * TOP:(i + 1) * TOP] for i in (1, 2, 3))
        weight = jnp.sum(jnp.where(match, weight, 0.0), axis=2)
        slot = jnp.dot(hit.astype(jnp.bfloat16), earlier, preferred_element_type=jnp.float32)
        pick = hit[:, None, :] & (slot[:, None, :] == slot_ids[None, :, None])
        row_weight = jnp.sum(jnp.where(pick, weight[:, None, :], 0.0), axis=2)
        return pick.astype(jnp.bfloat16), row_weight

    pick_own, weight_own = chosen_rows(own_facts, mine_expert)
    pick_other, _ = chosen_rows(own_facts, other_expert)
    _, weight_far = chosen_rows(far_facts, mine_expert)
    doc_ends = jnp.cumsum(lengths)
    lo = jnp.max(jnp.where(doc_ends[None, :] <= positions[:, None], doc_ends[None, :], 0), axis=1)
    heads_of = cols // HD
    my_sinks = lax.dynamic_index_in_dim(
        sinks.reshape(planes, PLANE, heads_of), in_plane, 1, keepdims=False
    ).reshape(-1)
    queries = make_queries(info, nb, cosine, sine, q_weights, planes, cols)
    attended = attend(
        info, lo[::tok_rows], my_sinks, queries, lo[:, None], positions[:, None],
        (own_kv, y_kv, c_kv, cy_kv), planes, cols,
    )
    send, keep = project(info, attended, w_out, wo_got, wo_twin, wo_ks)
    send, keep = add_core(keep, swap_with(send, "ctx", 1))
    mixed, expert_in = mix(tokens, keep, swap_with(send, "ctx", 2), moe_gain)

    def rows_for(pick, k, block):
        return jnp.dot(pick[k], block, preferred_element_type=jnp.float32).astype(jnp.bfloat16)

    def sent(k, block):
        rows = rows_for(pick_other, k, block)
        return rows, swap_with(rows, "ctx", 2)

    last = planes - 1
    near, far, ready = {}, {}, []
    first_rows, far[0] = sent(0, expert_in)
    blocks = over_planes(expert_in, planes)
    for k in range(planes - 1):
        near[k] = rows_for(pick_own, k, blocks[k])
        if k:
            rows, far[k] = sent(k, blocks[k])
            ready.append(rows)

    def run(parts):
        x = jnp.concatenate([rows for rows, _ in parts], axis=0)
        weights = jnp.concatenate([weight for _, weight in parts])
        out = expert(after(x, *ready), weights[:, None], slabs)
        return [out[i * padded:(i + 1) * padded] for i in range(len(parts))]

    done, back = {}, {}
    first = run([(near[k], weight_own[k]) for k in range(last)] + [(far[0], weight_far[0])])
    for k in range(last):
        done[k] = first[k]
    back[0] = swap_with(first[last], "ctx", 2)
    block = after(blocks[last], first[0])
    _, far[last] = sent(last, block)
    near[last] = rows_for(pick_own, last, block)
    middle = list(range(1, last))
    second = run(
        [(near[last], weight_own[last]), (far[last], weight_far[last])]
        + [(far[k], weight_far[k]) for k in middle]
    )
    done[last] = second[0]
    back[last] = swap_with(second[1], "ctx", 2)
    late = after(jnp.concatenate(second[2:], axis=0), back[last])
    late = swap_with(late, "ctx", 2)
    for i, k in enumerate(middle):
        back[k] = late[i * padded:(i + 1) * padded]

    def gathered(pick, k, rows):
        return lax.dot_general(
            pick[k], rows, (((0,), (0,)), ((), ())), preferred_element_type=jnp.float32
        )

    sums = {k: gathered(pick_own, k, done[k]) + gathered(pick_other, k, back[k]) for k in done}
    ends = []
    bit = 1
    while bit < planes:
        for k in sorted(sums, reverse=True):
            if k & bit:
                arrived = swap_with(sums.pop(k).astype(jnp.bfloat16), "ctx", PLANE * bit)
                if k ^ bit:
                    sums[k ^ bit] = sums[k ^ bit] + arrived.astype(jnp.float32)
                else:
                    ends.append(arrived)
        bit *= 2
    return finish(model_width, mixed, sums[0], *ends)


def solution(mesh):
    placed = (
        P(("groups", "ctx"), None),
        P("groups"),
        P(),
        P("ctx", None),
        P(),
        P(),
        P(),
        P("ctx", None),
        P(),
        P(("groups", "ctx"), None),
        P(("groups", "ctx"), None),
        P("ctx", None, None),
        P("ctx", None, None),
        P("ctx", None, None),
    )
    return jax.shard_map(
        per_device,
        mesh=mesh,
        in_specs=placed,
        out_specs=P(("groups", "ctx"), None),
        check_vma=False,
    )
```

profile of v0, /device:TPU:0, one launch (start us, length us, event | category | flops | bytes accessed | tf_op | source)
XLA Modules:
  0.0 315.9 jit_solution(851841928366889876)
XLA Ops:
  10.3 2.5 collective-permute-start.1
  18.6 3.8 %collective-permute-done.2.p3 = bf16[180,512]{1,0:T(8,128)(2,1)} collective-permute-done((bf16[180,512]{1,0:T(8,128)(2,1)}, bf16[180,512]{1,0:T(8,128)(2,1)}, u32[]{:S(2)}, u32[]{:S(2)}) %collective-permute-start.2) | collective-permute-done | bytes 184352 | tf_op jit(solution)/shard_map/ppermute | solution.py:23
  22.4 2.0 shard_map.156
  28.3 2.5 collective-permute-start.4
  31.7 2.3 copy.60.weight_ref.own_ref
  34.0 18.0 %collective-permute-done.5.refs_4_ = bf16[128,640]{1,0:T(8,128)(2,1)S(1)} collective-permute-done((bf16[128,640]{1,0:T(8,128)(2,1)S(1)}, bf16[128,640]{1,0:T(8,128)(2,1)S(1)}, u32[]{:S(2)}, u32[]{:S(2)}) %collective-permute-start.5) | collective-permute-done | bytes 163872 | tf_op jit(solution)/shard_map/ppermute | solution.py:23
  52.0 2.4 collective-permute-done.6.refs_5_
  56.2 2.0 shard_map.158.refs_11_
  60.0 2.7 collective-permute-start.8
  63.2 15.1 %collective-permute-done.11.refs_9_ = bf16[128,640]{1,0:T(8,128)(2,1)S(1)} collective-permute-done((bf16[128,640]{1,0:T(8,128)(2,1)S(1)}, bf16[128,640]{1,0:T(8,128)(2,1)S(1)}, u32[]{:S(2)}, u32[]{:S(2)}) %collective-permute-start.11) | collective-permute-done | bytes 163872 | tf_op jit(solution)/shard_map/ppermute | solution.py:23
  81.6 1.6 collective-permute-start.16
  85.7 2.4 shard_map.161.refs_1_
  88.1 1.7 copy-done
  93.9 2.1 collective-permute-done.17.refs_7_
  96.0 3.5 %collective-permute-done.15.refs_4_ = bf16[512,640]{1,0:T(8,128)(2,1)} collective-permute-done((bf16[512,640]{1,0:T(8,128)(2,1)S(1)}, bf16[512,640]{1,0:T(8,128)(2,1)}, u32[]{:S(2)}, u32[]{:S(2)}) %collective-permute-start.15) | collective-permute-done | bytes 655392 | tf_op jit(solution)/shard_map/ppermute | solution.py:23
  100.2 1.9 collective-permute-done.14.refs_2_
  106.3 7.1 %shard_map.166.refs_3_ = bf16[4,1024,128]{2,1,0:T(8,128)(2,1)} custom-call(s32[2]{0:T(128)} %copy-done.27, bf16[8,512,360]{2,1,0:T(8,128)(2,1)} %copy-done, f32[512,128]{1,0:T(8,128)} %copy-done.42, f32[512,128]{1,0:T(8,128)} %copy-done.41, bf16[360,512]{1,0:T(8,128)(2,1)} %get-tuple-element.70.refs_4_, bf16[360,512]{1,0:T(8,128)(2,1)} %copy-done.31, ...), custom_call_target="tpu_custom_call" | custom-call | flops 8000000000 | bytes 8000000 | tf_op jit(solution)/shard_map/pallas_call | solution.py:329
  115.2 9.0 %shard_map.167.att_ref = bf16[4,512,128]{2,1,0:T(8,128)(2,1)} custom-call(s32[2]{0:T(128)} %copy-done.27, s32[4]{0:T(128)} %slice.125.refs_1_, f32[8]{0:T(128)} %reshape.74.refs_2_, bf16[4,1024,128]{2,1,0:T(8,128)(2,1)} %shard_map.166.refs_3_, s32[512,1]{1,0:T(8,128)} %copy.61.refs_4_, s32[512,1]{1,0:T(8,128)} %copy.62.refs_5_, ...), custom_call_target="tpu_custom_call" | custom-call | flops 16000000000 | bytes 3674168 | tf_op jit(solution)/shard_map/pallas_call | solution.py:100
  125.3 3.5 %shard_map.168 = (bf16[256,2944]{1,0:T(8,128)(2,1)S(1)}, f32[256,2944]{1,0:T(8,128)S(1)}) custom-call(s32[2]{0:T(128)S(1)} %copy-done.28, bf16[4,512,128]{2,1,0:T(8,128)(2,1)S(1)} %copy-done.32, bf16[128,2880]{1,0:T(8,128)(2,1)S(1)} %copy-done.8, bf16[64,2944]{1,0:T(8,128)(2,1)S(1)} %copy-done.6, bf16[128,2944]{1,0:T(8,128)(2,1)} %get-tuple-element.89.rest_1_, ...), custom_call_target="tpu_custom_call" | custom-call | flops 4000000000 | bytes 3522568 | tf_op jit(solution)/shard_map/pallas_call | solution.py:100
  134.0 17.4 %collective-permute-done.22.got_ref = bf16[128,2944]{1,0:T(8,128)(2,1)S(1)} collective-permute-done((bf16[128,2944]{1,0:T(8,128)(2,1)S(1)}, bf16[128,2944]{1,0:T(8,128)(2,1)S(1)}, u32[]{:S(2)}, u32[]{:S(2)}) %collective-permute-start.22) | collective-permute-done | bytes 753696 | tf_op jit(solution)/shard_map/ppermute | solution.py:23
  151.9 8.1 %collective-permute-start.24 = (bf16[128,2944]{1,0:T(8,128)(2,1)S(1)}, bf16[128,2944]{1,0:T(8,128)(2,1)S(1)}, u32[]{:S(2)}, u32[]{:S(2)}) collective-permute-start(bf16[128,2944]{1,0:T(8,128)(2,1)S(1)} %get-tuple-element.96), channel_id=1, source_target_pairs={{0,8},{1,9},{2,10},{3,11},{4,12},{5,13},{6,14},{7,15},{8,0},{9,1},... | collective-permute-start | bytes 2261000 | tf_op jit(solution)/shard_map/ppermute | solution.py:23
  162.9 27.3 %collective-permute-done.24 = bf16[128,2944]{1,0:T(8,128)(2,1)S(1)} collective-permute-done((bf16[128,2944]{1,0:T(8,128)(2,1)S(1)}, bf16[128,2944]{1,0:T(8,128)(2,1)S(1)}, u32[]{:S(2)}, u32[]{:S(2)}) %collective-permute-start.24) | collective-permute-done | bytes 753696 | tf_op jit(solution)/shard_map/ppermute | solution.py:23
  191.7 4.1 %collective-permute-done.23 = bf16[128,2944]{1,0:T(8,128)(2,1)S(1)} collective-permute-done((bf16[128,2944]{1,0:T(8,128)(2,1)S(1)}, bf16[128,2944]{1,0:T(8,128)(2,1)S(1)}, u32[]{:S(2)}, u32[]{:S(2)}) %collective-permute-start.23) | collective-permute-done | bytes 753696 | tf_op jit(solution)/shard_map/ppermute | solution.py:23
  198.2 12.2 %collective-permute-done.27 = bf16[128,2944]{1,0:T(8,128)(2,1)S(1)} collective-permute-done((bf16[128,2944]{1,0:T(8,128)(2,1)S(1)}, bf16[128,2944]{1,0:T(8,128)(2,1)S(1)}, u32[]{:S(2)}, u32[]{:S(2)}) %collective-permute-start.27) | collective-permute-done | bytes 753696 | tf_op jit(solution)/shard_map/ppermute | solution.py:23
  213.2 7.9 %collective-permute-done.28 = bf16[72,2944]{1,0:T(8,128)(2,1)S(1)} collective-permute-done((bf16[72,2944]{1,0:T(8,128)(2,1)S(1)}, bf16[72,2944]{1,0:T(8,128)(2,1)S(1)}, u32[]{:S(2)}, u32[]{:S(2)}) %collective-permute-start.28) | collective-permute-done | bytes 423968 | tf_op jit(solution)/shard_map/ppermute | solution.py:23
  221.4 23.5 %shard_map.172 = bf16[288,2944]{1,0:T(8,128)(2,1)S(1)} custom-call(bf16[288,2944]{1,0:T(8,128)(2,1)S(1)} %pad_maximum_fusion.1.x_ref, f32[288,1]{1,0:T(8,128)S(1)} %broadcast_in_dim.80.row_ref, bf16[2,2880,768]{2,1,0:T(8,128)(2,1)} %all-gather.4.cloned.1.call-done.gate_ref, bf16[2,2880,768]{2,1,0:T(8,128)(2,1)} %all-gather.6.cloned.1.call-done.up_ref, ...), custom_call_target="tpu_custom_call" | custom-call | flops 7644119040 | bytes 26542080 | tf_op jit(solution)/shard_map/pallas_call | solution.py:634
  247.6 6.7 %collective-permute-done.31 = bf16[72,2944]{1,0:T(8,128)(2,1)S(1)} collective-permute-done((bf16[72,2944]{1,0:T(8,128)(2,1)S(1)}, bf16[72,2944]{1,0:T(8,128)(2,1)S(1)}, u32[]{:S(2)}, u32[]{:S(2)}) %collective-permute-start.31) | collective-permute-done | bytes 423968 | tf_op jit(solution)/shard_map/ppermute | solution.py:23
  254.7 2.0 collective-permute-start.34
  257.9 13.7 %shard_map.171 = bf16[288,2944]{1,0:T(8,128)(2,1)S(1)} custom-call(bf16[288,2944]{1,0:T(8,128)(2,1)S(1)} %pad_maximum_fusion.x_ref, f32[288,1]{1,0:T(8,128)S(1)} %broadcast_in_dim.79.row_ref, bf16[2,2880,768]{2,1,0:T(8,128)(2,1)} %all-gather.4.cloned.1.call-done.gate_ref, bf16[2,2880,768]{2,1,0:T(8,128)(2,1)} %all-gather.6.cloned.1.call-done.up_ref, ...), custom_call_target="tpu_custom_call" | custom-call | flops 7644119040 | bytes 26542080 | tf_op jit(solution)/shard_map/pallas_call | solution.py:634
  272.4 2.6 collective-permute-done.32
  278.0 6.7 %collective-permute-done.26 = bf16[72,2944]{1,0:T(8,128)(2,1)S(1)} collective-permute-done((bf16[72,2944]{1,0:T(8,128)(2,1)S(1)}, bf16[72,2944]{1,0:T(8,128)(2,1)S(1)}, u32[]{:S(2)}, u32[]{:S(2)}) %collective-permute-start.26) | collective-permute-done | bytes 423968 | tf_op jit(solution)/shard_map/ppermute | solution.py:23
  285.2 22.7 %collective-permute-done.35.rest_1_ = bf16[128,2944]{1,0:T(8,128)(2,1)S(1)} collective-permute-done((bf16[128,2944]{1,0:T(8,128)(2,1)S(1)}, bf16[128,2944]{1,0:T(8,128)(2,1)S(1)}, u32[]{:S(2)}, u32[]{:S(2)}) %collective-permute-start.35) | collective-permute-done | bytes 753696 | tf_op jit(solution)/shard_map/ppermute | solution.py:23
  (234 shorter events, 60.6 us)
Async XLA Ops:
  6.5 214.7 %all-gather.4.cloned.1.call-start = ((), (), s32[]{:S(2)}) async-start(), calls=%async_computation | async-start | bytes 13271040 | tf_op jit(solution)/shard_map/all_gather | solution.py:680
  7.3 214.0 %all-gather.6.cloned.1.call-start = ((), (), s32[]{:S(2)}) async-start(), calls=%async_computation.1 | async-start | bytes 13271040 | tf_op jit(solution)/shard_map/all_gather | solution.py:680
  8.1 213.2 %all-gather.8.cloned.1.call-start = ((), (), s32[]{:S(2)}) async-start(), calls=%async_computation.2 | async-start | bytes 13271040 | tf_op jit(solution)/shard_map/all_gather | solution.py:680
  25.2 29.3 %collective-permute-start.7 = (bf16[128,2944]{1,0:T(8,128)(2,1)}, bf16[128,2944]{1,0:T(8,128)(2,1)S(1)}, u32[]{:S(2)}, u32[]{:S(2)}) collective-permute-start(bf16[128,2944]{1,0:T(8,128)(2,1)} %get-tuple-element.61), channel_id=1, source_target_pairs={{0,2},{1,3},{2,0},{3,1},{4,6},{5,7},{6,4},{7,5},{8,10},{9,11},{10,... | collective-permute-start | bytes 2261000 | tf_op jit(solution)/shard_map/ppermute | solution.py:23
  26.8 27.6 %collective-permute-start.3 = (bf16[360,512]{1,0:T(8,128)(2,1)S(1)}, bf16[360,512]{1,0:T(8,128)(2,1)S(1)}, u32[]{:S(2)}, u32[]{:S(2)}) collective-permute-start(bf16[360,512]{1,0:T(8,128)(2,1)S(1)} %get-tuple-element.59.refs_0_), channel_id=1, source_target_pairs={{0,4},{1,5},{2,6},{3,7},{4,0},{5,1},{6,2},{7,3},{8,12},{9,13},{10,... | collective-permute-start | bytes 1105928 | tf_op jit(solution)/shard_map/ppermute | solution.py:23
  28.3 26.1 %collective-permute-start.4 = (bf16[360,512]{1,0:T(8,128)(2,1)S(1)}, bf16[360,512]{1,0:T(8,128)(2,1)S(1)}, u32[]{:S(2)}, u32[]{:S(2)}) collective-permute-start(bf16[360,512]{1,0:T(8,128)(2,1)S(1)} %get-tuple-element.59.refs_0_), channel_id=1, source_target_pairs={{0,8},{1,9},{2,10},{3,11},{4,12},{5,13},{6,14},{7,15},{8,0},{9,1},... | collective-permute-start | bytes 1105928 | tf_op jit(solution)/shard_map/ppermute | solution.py:23
  30.9 21.1 %collective-permute-start.5 = (bf16[128,640]{1,0:T(8,128)(2,1)S(1)}, bf16[128,640]{1,0:T(8,128)(2,1)S(1)}, u32[]{:S(2)}, u32[]{:S(2)}) collective-permute-start(bf16[128,640]{1,0:T(8,128)(2,1)S(1)} %get-tuple-element.60.refs_3_), channel_id=1, source_target_pairs={{0,4},{1,5},{2,6},{3,7},{4,0},{5,1},{6,2},{7,3},{8,12},{9,13},{10,... | collective-permute-start | bytes 491528 | tf_op jit(solution)/shard_map/ppermute | solution.py:23
  31.3 23.0 %collective-permute-start.6 = (bf16[128,640]{1,0:T(8,128)(2,1)S(1)}, bf16[128,640]{1,0:T(8,128)(2,1)S(1)}, u32[]{:S(2)}, u32[]{:S(2)}) collective-permute-start(bf16[128,640]{1,0:T(8,128)(2,1)S(1)} %get-tuple-element.60.refs_3_), channel_id=1, source_target_pairs={{0,8},{1,9},{2,10},{3,11},{4,12},{5,13},{6,14},{7,15},{8,0},{9,1},... | collective-permute-start | bytes 491528 | tf_op jit(solution)/shard_map/ppermute | solution.py:23
  58.2 20.1 %collective-permute-start.12 = (bf16[64,2944]{1,0:T(8,128)(2,1)}, bf16[64,2944]{1,0:T(8,128)(2,1)S(1)}, u32[]{:S(2)}, u32[]{:S(2)}) collective-permute-start(bf16[64,2944]{1,0:T(8,128)(2,1)} %shard_map.158.refs_11_), channel_id=1, source_target_pairs={{0,8},{1,9},{2,10},{3,11},{4,12},{5,13},{6,14},{7,15},{8,0},{9,1},... | collective-permute-start | bytes 1130504 | tf_op jit(solution)/shard_map/ppermute | solution.py:23
  58.5 19.8 %collective-permute-start.10 = (bf16[360,512]{1,0:T(8,128)(2,1)S(1)}, bf16[360,512]{1,0:T(8,128)(2,1)S(1)}, u32[]{:S(2)}, u32[]{:S(2)}) collective-permute-start(bf16[360,512]{1,0:T(8,128)(2,1)S(1)} %copy-done.38), channel_id=1, source_target_pairs={{0,16},{16,0},{1,17},{17,1},{2,18},{18,2},{3,19},{19,3},{4,20},{20... | collective-permute-start | bytes 1105928 | tf_op jit(solution)/shard_map/ppermute | solution.py:23
  60.0 18.3 %collective-permute-start.8 = (bf16[360,512]{1,0:T(8,128)(2,1)S(1)}, bf16[360,512]{1,0:T(8,128)(2,1)}, u32[]{:S(2)}, u32[]{:S(2)}) collective-permute-start(bf16[360,512]{1,0:T(8,128)(2,1)S(1)} %copy-done.38), channel_id=1, source_target_pairs={{0,4},{1,5},{2,6},{3,7},{4,0},{5,1},{6,2},{7,3},{8,12},{9,13},{10,... | collective-permute-start | bytes 1105928 | tf_op jit(solution)/shard_map/ppermute | solution.py:23
  62.7 15.6 %collective-permute-start.9 = (bf16[360,512]{1,0:T(8,128)(2,1)S(1)}, bf16[360,512]{1,0:T(8,128)(2,1)S(1)}, u32[]{:S(2)}, u32[]{:S(2)}) collective-permute-start(bf16[360,512]{1,0:T(8,128)(2,1)S(1)} %copy-done.36), channel_id=1, source_target_pairs={{0,16},{16,0},{1,17},{17,1},{2,18},{18,2},{3,19},{19,3},{4,20},{20... | collective-permute-start | bytes 1105928 | tf_op jit(solution)/shard_map/ppermute | solution.py:23
  63.2 15.1 %collective-permute-start.11 = (bf16[128,640]{1,0:T(8,128)(2,1)S(1)}, bf16[128,640]{1,0:T(8,128)(2,1)S(1)}, u32[]{:S(2)}, u32[]{:S(2)}) collective-permute-start(bf16[128,640]{1,0:T(8,128)(2,1)S(1)} %copy-done.14), channel_id=1, source_target_pairs={{0,4},{1,5},{2,6},{3,7},{4,0},{5,1},{6,2},{7,3},{8,12},{9,13},{10,... | collective-permute-start | bytes 491528 | tf_op jit(solution)/shard_map/ppermute | solution.py:23
  81.6 18.5 %collective-permute-start.16 = (bf16[128,2944]{1,0:T(8,128)(2,1)S(1)}, bf16[128,2944]{1,0:T(8,128)(2,1)}, u32[]{:S(2)}, u32[]{:S(2)}) collective-permute-start(bf16[128,2944]{1,0:T(8,128)(2,1)S(1)} %shard_map.164), channel_id=1, source_target_pairs={{0,4},{1,5},{2,6},{3,7},{4,0},{5,1},{6,2},{7,3},{8,12},{9,13},{10,... | collective-permute-start | bytes 2261000 | tf_op jit(solution)/shard_map/ppermute | solution.py:23
  83.4 16.1 %collective-permute-start.15 = (bf16[512,640]{1,0:T(8,128)(2,1)S(1)}, bf16[512,640]{1,0:T(8,128)(2,1)}, u32[]{:S(2)}, u32[]{:S(2)}) collective-permute-start(bf16[512,640]{1,0:T(8,128)(2,1)S(1)} %shard_map.163.refs_3_), channel_id=1, source_target_pairs={{0,2},{1,3},{2,0},{3,1},{4,6},{5,7},{6,4},{7,5},{8,10},{9,11},{10,... | collective-permute-start | bytes 1966088 | tf_op jit(solution)/shard_map/ppermute | solution.py:23
  84.2 11.8 %collective-permute-start.17 = (bf16[64,2944]{1,0:T(8,128)(2,1)S(1)}, bf16[64,2944]{1,0:T(8,128)(2,1)}, u32[]{:S(2)}, u32[]{:S(2)}) collective-permute-start(bf16[64,2944]{1,0:T(8,128)(2,1)S(1)} %copy-done.5), channel_id=1, source_target_pairs={{0,16},{16,0},{1,17},{17,1},{2,18},{18,2},{3,19},{19,3},{4,20},{20... | collective-permute-start | bytes 1130504 | tf_op jit(solution)/shard_map/ppermute | solution.py:23
  89.9 12.2 %collective-permute-start.14 = (bf16[360,512]{1,0:T(8,128)(2,1)}, bf16[360,512]{1,0:T(8,128)(2,1)S(1)}, u32[]{:S(2)}, u32[]{:S(2)}) collective-permute-start(bf16[360,512]{1,0:T(8,128)(2,1)} %shard_map.162.refs_10_), channel_id=1, source_target_pairs={{0,16},{16,0},{1,17},{17,1},{2,18},{18,2},{3,19},{19,3},{4,20},{20... | collective-permute-start | bytes 1105928 | tf_op jit(solution)/shard_map/ppermute | solution.py:23
  102.9 10.6 %collective-permute-start.18 = (bf16[512,640]{1,0:T(8,128)(2,1)}, bf16[512,640]{1,0:T(8,128)(2,1)S(1)}, u32[]{:S(2)}, u32[]{:S(2)}) collective-permute-start(bf16[512,640]{1,0:T(8,128)(2,1)} %get-tuple-element.86.refs_6_), channel_id=1, source_target_pairs={{0,1},{1,0},{2,3},{3,2},{4,5},{5,4},{6,7},{7,6},{8,9},{9,8},{10,11... | collective-permute-start | bytes 1966088 | tf_op jit(solution)/shard_map/ppermute | solution.py:23
  102.9 10.7 %collective-permute-start.19 = (bf16[512,640]{1,0:T(8,128)(2,1)}, bf16[512,640]{1,0:T(8,128)(2,1)S(1)}, u32[]{:S(2)}, u32[]{:S(2)}) collective-permute-start(bf16[512,640]{1,0:T(8,128)(2,1)} %get-tuple-element.87.refs_7_), channel_id=1, source_target_pairs={{0,1},{1,0},{2,3},{3,2},{4,5},{5,4},{6,7},{7,6},{8,9},{9,8},{10,11... | collective-permute-start | bytes 1966088 | tf_op jit(solution)/shard_map/ppermute | solution.py:23
  103.4 20.9 %collective-permute-start.20 = (bf16[128,2944]{1,0:T(8,128)(2,1)}, bf16[128,2944]{1,0:T(8,128)(2,1)S(1)}, u32[]{:S(2)}, u32[]{:S(2)}) collective-permute-start(bf16[128,2944]{1,0:T(8,128)(2,1)} %get-tuple-element.89.rest_1_), channel_id=1, source_target_pairs={{0,16},{16,0},{1,17},{17,1},{2,18},{18,2},{3,19},{19,3},{4,20},{20... | collective-permute-start | bytes 2261000 | tf_op jit(solution)/shard_map/ppermute | solution.py:23
  132.5 18.9 %collective-permute-start.22 = (bf16[128,2944]{1,0:T(8,128)(2,1)S(1)}, bf16[128,2944]{1,0:T(8,128)(2,1)S(1)}, u32[]{:S(2)}, u32[]{:S(2)}) collective-permute-start(bf16[128,2944]{1,0:T(8,128)(2,1)S(1)} %get-tuple-element.94), channel_id=1, source_target_pairs={{0,2},{1,3},{2,0},{3,1},{4,6},{5,7},{6,4},{7,5},{8,10},{9,11},{10,... | collective-permute-start | bytes 2261000 | tf_op jit(solution)/shard_map/ppermute | solution.py:23
  151.9 38.3 %collective-permute-start.24 = (bf16[128,2944]{1,0:T(8,128)(2,1)S(1)}, bf16[128,2944]{1,0:T(8,128)(2,1)S(1)}, u32[]{:S(2)}, u32[]{:S(2)}) collective-permute-start(bf16[128,2944]{1,0:T(8,128)(2,1)S(1)} %get-tuple-element.96), channel_id=1, source_target_pairs={{0,8},{1,9},{2,10},{3,11},{4,12},{5,13},{6,14},{7,15},{8,0},{9,1},... | collective-permute-start | bytes 2261000 | tf_op jit(solution)/shard_map/ppermute | solution.py:23
  160.4 35.4 %collective-permute-start.23 = (bf16[128,2944]{1,0:T(8,128)(2,1)S(1)}, bf16[128,2944]{1,0:T(8,128)(2,1)S(1)}, u32[]{:S(2)}, u32[]{:S(2)}) collective-permute-start(bf16[128,2944]{1,0:T(8,128)(2,1)S(1)} %get-tuple-element.96), channel_id=1, source_target_pairs={{0,4},{1,5},{2,6},{3,7},{4,0},{5,1},{6,2},{7,3},{8,12},{9,13},{10,... | collective-permute-start | bytes 2261000 | tf_op jit(solution)/shard_map/ppermute | solution.py:23
  161.5 84.5 %collective-permute-start.25 = (bf16[72,2944]{1,0:T(8,128)(2,1)}, bf16[72,2944]{1,0:T(8,128)(2,1)}, u32[]{:S(2)}, u32[]{:S(2)}) collective-permute-start(bf16[72,2944]{1,0:T(8,128)(2,1)} %convolution_convert_fusion.4), channel_id=1, source_target_pairs={{0,2},{1,3},{2,0},{3,1},{4,6},{5,7},{6,4},{7,5},{8,10},{9,11},{10,... | collective-permute-start | bytes 1271816 | tf_op jit(solution)/shard_map/ppermute | solution.py:23
  190.2 20.2 %collective-permute-start.27 = (bf16[128,2944]{1,0:T(8,128)(2,1)S(1)}, bf16[128,2944]{1,0:T(8,128)(2,1)S(1)}, u32[]{:S(2)}, u32[]{:S(2)}) collective-permute-start(bf16[128,2944]{1,0:T(8,128)(2,1)S(1)} %collective-permute-done.24), channel_id=1, source_target_pairs={{0,4},{1,5},{2,6},{3,7},{4,0},{5,1},{6,2},{7,3},{8,12},{9,13},{10,... | collective-permute-start | bytes 2261000 | tf_op jit(solution)/shard_map/ppermute | solution.py:23
  190.5 22.7 %collective-permute-start.30 = (bf16[72,2944]{1,0:T(8,128)(2,1)S(1)}, bf16[72,2944]{1,0:T(8,128)(2,1)S(1)}, u32[]{:S(2)}, u32[]{:S(2)}) collective-permute-start(bf16[72,2944]{1,0:T(8,128)(2,1)S(1)} %convolution_convert_fusion.2), channel_id=1, source_target_pairs={{0,2},{1,3},{2,0},{3,1},{4,6},{5,7},{6,4},{7,5},{8,10},{9,11},{10,... | collective-permute-start | bytes 1271816 | tf_op jit(solution)/shard_map/ppermute | solution.py:23
  196.1 17.2 %collective-permute-start.29 = (bf16[72,2944]{1,0:T(8,128)(2,1)S(1)}, bf16[72,2944]{1,0:T(8,128)(2,1)S(1)}, u32[]{:S(2)}, u32[]{:S(2)}) collective-permute-start(bf16[72,2944]{1,0:T(8,128)(2,1)S(1)} %convolution_convert_fusion.3), channel_id=1, source_target_pairs={{0,2},{1,3},{2,0},{3,1},{4,6},{5,7},{6,4},{7,5},{8,10},{9,11},{10,... | collective-permute-start | bytes 1271816 | tf_op jit(solution)/shard_map/ppermute | solution.py:23
  210.7 10.4 %collective-permute-start.28 = (bf16[72,2944]{1,0:T(8,128)(2,1)S(1)}, bf16[72,2944]{1,0:T(8,128)(2,1)S(1)}, u32[]{:S(2)}, u32[]{:S(2)}) collective-permute-start(bf16[72,2944]{1,0:T(8,128)(2,1)S(1)} %convolution_convert_fusion), channel_id=1, source_target_pairs={{0,2},{1,3},{2,0},{3,1},{4,6},{5,7},{6,4},{7,5},{8,10},{9,11},{10,... | collective-permute-start | bytes 1271816 | tf_op jit(solution)/shard_map/ppermute | solution.py:23
  254.7 17.6 %collective-permute-start.34 = (bf16[128,2944]{1,0:T(8,128)(2,1)S(1)}, bf16[128,2944]{1,0:T(8,128)(2,1)S(1)}, u32[]{:S(2)}, u32[]{:S(2)}) collective-permute-start(bf16[128,2944]{1,0:T(8,128)(2,1)S(1)} %fusion.3), channel_id=1, source_target_pairs={{0,4},{1,5},{2,6},{3,7},{4,0},{5,1},{6,2},{7,3},{8,12},{9,13},{10,... | collective-permute-start | bytes 2261000 | tf_op jit(solution)/shard_map/ppermute | solution.py:23
  256.8 18.2 %collective-permute-start.32 = (bf16[144,2944]{1,0:T(8,128)(2,1)S(1)}, bf16[144,2944]{1,0:T(8,128)(2,1)S(1)}, u32[]{:S(2)}, u32[]{:S(2)}) collective-permute-start(bf16[144,2944]{1,0:T(8,128)(2,1)S(1)} %concatenate.28), channel_id=1, source_target_pairs={{0,2},{1,3},{2,0},{3,1},{4,6},{5,7},{6,4},{7,5},{8,10},{9,11},{10,... | collective-permute-start | bytes 2543624 | tf_op jit(solution)/shard_map/ppermute | solution.py:23
  275.5 32.4 %collective-permute-start.35 = (bf16[128,2944]{1,0:T(8,128)(2,1)S(1)}, bf16[128,2944]{1,0:T(8,128)(2,1)S(1)}, u32[]{:S(2)}, u32[]{:S(2)}) collective-permute-start(bf16[128,2944]{1,0:T(8,128)(2,1)S(1)} %fusion.2), channel_id=1, source_target_pairs={{0,8},{1,9},{2,10},{3,11},{4,12},{5,13},{6,14},{7,15},{8,0},{9,1},... | collective-permute-start | bytes 2261000 | tf_op jit(solution)/shard_map/ppermute | solution.py:23
  276.0 31.9 %collective-permute-start.33 = (bf16[128,2944]{1,0:T(8,128)(2,1)S(1)}, bf16[128,2944]{1,0:T(8,128)(2,1)S(1)}, u32[]{:S(2)}, u32[]{:S(2)}) collective-permute-start(bf16[128,2944]{1,0:T(8,128)(2,1)S(1)} %fusion.1), channel_id=1, source_target_pairs={{0,4},{1,5},{2,6},{3,7},{4,0},{5,1},{6,2},{7,3},{8,12},{9,13},{10,... | collective-permute-start | bytes 2261000 | tf_op jit(solution)/shard_map/ppermute | solution.py:23
  (59 other events, 347.8 us)
Sparse Core Ops, SparseCore 0:
  8.9 23.8 all-gather.3
  34.4 22.3 all-gather.5
  84.1 22.4 all-gather.7
where the time goes:
time: 320 us; the launch traced here: 316 us
  waiting for transfers between devices  158 us (49%)
  Pallas kernels  68.1 us (21%)
  starting transfers between devices  41 us (13%)
  local copies, waits for them, and re-layouts  20 us (6%)
  between operations  14.1 us (4%)
  matrix products  8.22 us (3%)
  other arithmetic  6.22 us (2%)
    ppermute x36, waiting for transfers between devices, swap_with(): lax.ppermute(x, axis, [(i, i ^ bits) for i in range(lax.axis_size(axis))])  157 us
    ppermute x36, starting transfers between devices, swap_with(): lax.ppermute(x, axis, [(i, i ^ bits) for i in range(lax.axis_size(axis))])  40.9 us
    pallas_call x2, Pallas kernels, expert(): pl.pallas_call(body, out_shape=jax.ShapeDtypeStruct((rows, padded), jnp.b...  37.1 us
    pallas_call x12, Pallas kernels, whole_call(): pl.pallas_call(body, out_shape=out_shapes, in_specs=[smem] * scalars + [v...  21.8 us
    unnamed x105, local copies, waits for them, and re-layouts  16.5 us
    pallas_call x1, Pallas kernels, make_queries(): pl.pallas_call(body, out_shape=jax.ShapeDtypeStruct((kv_heads, 2 * rows,...  7.15 us
  transfers between devices with their start and end apart: 39, of which 19 were waited for; matrix products, arithmetic and copies ran while one was open for 6% of the time, Pallas kernels for 21%

commit v1 on v0

--- a/solution.py
+++ b/solution.py
@@ -35,7 +35,6 @@
         in_specs=[anywhere] * (1 + len(earlier)),
         out_specs=anywhere,
         input_output_aliases={0: 0},
-        compiler_params=pltpu.CompilerParams(vmem_limit_bytes=60 * 1024 * 1024),
     )(value, *earlier)
 
 
@@ -601,33 +600,46 @@
     rows, padded = x.shape
     width, hidden = slabs[0].shape[1:]
 
-    def body(x_ref, row_ref, gate_ref, up_ref, down_ref, out_ref, held, sem):
+    def body(x_ref, row_ref, gate_ref, up_ref, down_ref, out_ref, held, acc, sem):
         copies = [
             pltpu.make_async_copy(ref.at[side], held.at[3 * side + i], sem.at[3 * side + i])
             for side in range(2)
             for i, ref in enumerate((gate_ref, up_ref, down_ref))
         ]
-        for copy in copies[:2]:
+        for copy in copies[:3]:
             copy.start()
-        total = None
-        for side in range(2):
-            i = 3 * side
+
+        def wait(side, i):
+            for s in range(2):
+                @pl.when(side == s)
+                def _():
+                    copies[3 * s + i].wait()
+                    if s == 0:
+                        copies[3 + i].start()
+
+        def one_slab(side, carry):
             inputs = x_ref[:, :width]
-            copies[i].wait()
-            copies[i + 2].start()
-            gate_val = jnp.dot(inputs, held[i], preferred_element_type=jnp.float32)
-            copies[i + 1].wait()
-            if side == 0:
-                copies[3].start()
-                copies[4].start()
-            up_val = jnp.dot(inputs, held[i + 1], preferred_element_type=jnp.float32)
+            wait(side, 0)
+            gate_val = jnp.dot(inputs, held[3 * side], preferred_element_type=jnp.float32)
+            wait(side, 1)
+            up_val = jnp.dot(inputs, held[3 * side + 1], preferred_element_type=jnp.float32)
             rows_in = ((up_val + 1.0) * gate_val * jax.nn.sigmoid(ALPHA * gate_val)).astype(
                 jnp.bfloat16
             )
-            copies[i + 2].wait()
-            term = by_columns(rows_in, held[i + 2])
-            total = term if total is None else total + term
-        out_ref[:, :width] = (total * row_ref[...]).astype(jnp.bfloat16)
+            wait(side, 2)
+            term = by_columns(rows_in, held[3 * side + 2])
+
+            @pl.when(side == 0)
+            def _():
+                acc[...] = term
+
+            @pl.when(side == 1)
+            def _():
+                out_ref[:, :width] = ((acc[...] + term) * row_ref[...]).astype(jnp.bfloat16)
+
+            return carry
+
+        lax.fori_loop(0, 2, one_slab, 0)
         out_ref[:, width:] = jnp.zeros((rows, padded - width), jnp.bfloat16)
 
     vmem = pl.BlockSpec(memory_space=pltpu.VMEM)
@@ -638,6 +650,7 @@
         out_specs=vmem,
         scratch_shapes=[
             pltpu.VMEM((6, width, hidden), jnp.bfloat16),
+            pltpu.VMEM((rows, width), jnp.float32),
             pltpu.SemaphoreType.DMA((6,)),
         ],
         compiler_params=pltpu.CompilerParams(vmem_limit_bytes=48 * 1024 * 1024),

time: 320 us -> 311 us (0.972); the launches traced: 316 us -> 310 us
  Pallas kernels: 68.1 us -> 59.5 us
  starting transfers between devices: 41 us -> 48.8 us
  waiting for transfers between devices: 158 us -> 154 us
    pallas_call x2, Pallas kernels: 37.1 us -> 28.6 us  [expert(): pl.pallas_call(body, out_shape=jax.ShapeDtypeStruct((rows, padded), jnp.b...]
    ppermute x36, starting transfers between devices: 40.9 us -> 48.8 us  [swap_with(): lax.ppermute(x, axis, [(i, i ^ bits) for i in range(lax.axis_size(axis))])]
    ppermute x36, waiting for transfers between devices: 157 us -> 152 us  [swap_with(): lax.ppermute(x, axis, [(i, i ^ bits) for i in range(lax.axis_size(axis))])]
  transfers between devices with their start and end apart: 39 -> 39, of which waited for: 19 -> 21; matrix products, arithmetic and copies ran while one was open for 6% -> 6% of each run, Pallas kernels for 21% -> 19%
where the time goes in v1:
time: 311 us; the launch traced here: 310 us
  waiting for transfers between devices  154 us (50%)
  Pallas kernels  59.5 us (19%)
  starting transfers between devices  48.8 us (16%)
  local copies, waits for them, and re-layouts  20 us (6%)
  between operations  13.9 us (4%)
  matrix products  8.21 us (3%)
  other arithmetic  6.22 us (2%)
    ppermute x36, waiting for transfers between devices, swap_with(): lax.ppermute(x, axis, [(i, i ^ bits) for i in range(lax.axis_size(axis))])  152 us
    ppermute x36, starting transfers between devices, swap_with(): lax.ppermute(x, axis, [(i, i ^ bits) for i in range(lax.axis_size(axis))])  48.8 us
    pallas_call x2, Pallas kernels, expert(): pl.pallas_call(body, out_shape=jax.ShapeDtypeStruct((rows, padded), jnp.b...  28.6 us
    pallas_call x12, Pallas kernels, whole_call(): pl.pallas_call(body, out_shape=out_shapes, in_specs=[smem] * scalars + [v...  21.8 us
    unnamed x105, local copies, waits for them, and re-layouts  16.5 us
    pallas_call x1, Pallas kernels, make_queries(): pl.pallas_call(body, out_shape=jax.ShapeDtypeStruct((kv_heads, 2 * rows,...  7.14 us
  transfers between devices with their start and end apart: 39, of which 21 were waited for; matrix products, arithmetic and copies ran while one was open for 6% of the time, Pallas kernels for 19%

profile of v1, /device:TPU:0, one launch (start us, length us, event | category | flops | bytes accessed | tf_op | source)
XLA Modules:
  0.0 310.3 jit_solution(649691728778017717)
XLA Ops:
  10.3 2.5 collective-permute-start.1
  18.6 3.8 %collective-permute-done.2.p3 = bf16[180,512]{1,0:T(8,128)(2,1)} collective-permute-done((bf16[180,512]{1,0:T(8,128)(2,1)}, bf16[180,512]{1,0:T(8,128)(2,1)}, u32[]{:S(2)}, u32[]{:S(2)}) %collective-permute-start.2) | collective-permute-done | bytes 184352 | tf_op jit(solution)/shard_map/ppermute | solution.py:23
  22.4 2.0 shard_map.156
  28.3 2.5 collective-permute-start.4
  31.7 2.3 copy.60.weight_ref.own_ref
  34.0 18.0 %collective-permute-done.5.refs_4_ = bf16[128,640]{1,0:T(8,128)(2,1)S(1)} collective-permute-done((bf16[128,640]{1,0:T(8,128)(2,1)S(1)}, bf16[128,640]{1,0:T(8,128)(2,1)S(1)}, u32[]{:S(2)}, u32[]{:S(2)}) %collective-permute-start.5) | collective-permute-done | bytes 163872 | tf_op jit(solution)/shard_map/ppermute | solution.py:23
  52.0 2.4 collective-permute-done.6.refs_5_
  56.2 2.0 shard_map.158.refs_11_
  60.0 2.7 collective-permute-start.8
  63.2 15.1 %collective-permute-done.11.refs_9_ = bf16[128,640]{1,0:T(8,128)(2,1)S(1)} collective-permute-done((bf16[128,640]{1,0:T(8,128)(2,1)S(1)}, bf16[128,640]{1,0:T(8,128)(2,1)S(1)}, u32[]{:S(2)}, u32[]{:S(2)}) %collective-permute-start.11) | collective-permute-done | bytes 163872 | tf_op jit(solution)/shard_map/ppermute | solution.py:23
  85.7 2.4 shard_map.161.refs_1_
  88.1 1.7 copy-done
  93.9 2.1 collective-permute-done.17.refs_7_
  96.0 3.5 %collective-permute-done.15.refs_4_ = bf16[512,640]{1,0:T(8,128)(2,1)} collective-permute-done((bf16[512,640]{1,0:T(8,128)(2,1)S(1)}, bf16[512,640]{1,0:T(8,128)(2,1)}, u32[]{:S(2)}, u32[]{:S(2)}) %collective-permute-start.15) | collective-permute-done | bytes 655392 | tf_op jit(solution)/shard_map/ppermute | solution.py:23
  100.2 1.9 collective-permute-done.14.refs_2_
  106.3 7.1 %shard_map.166.refs_3_ = bf16[4,1024,128]{2,1,0:T(8,128)(2,1)} custom-call(s32[2]{0:T(128)} %copy-done.27, bf16[8,512,360]{2,1,0:T(8,128)(2,1)} %copy-done, f32[512,128]{1,0:T(8,128)} %copy-done.42, f32[512,128]{1,0:T(8,128)} %copy-done.41, bf16[360,512]{1,0:T(8,128)(2,1)} %get-tuple-element.70.refs_4_, bf16[360,512]{1,0:T(8,128)(2,1)} %copy-done.31, ...), custom_call_target="tpu_custom_call" | custom-call | flops 8000000000 | bytes 8000000 | tf_op jit(solution)/shard_map/pallas_call | solution.py:328
  115.2 9.0 %shard_map.167.att_ref = bf16[4,512,128]{2,1,0:T(8,128)(2,1)} custom-call(s32[2]{0:T(128)} %copy-done.27, s32[4]{0:T(128)} %slice.125.refs_1_, f32[8]{0:T(128)} %reshape.74.refs_2_, bf16[4,1024,128]{2,1,0:T(8,128)(2,1)} %shard_map.166.refs_3_, s32[512,1]{1,0:T(8,128)} %copy.61.refs_4_, s32[512,1]{1,0:T(8,128)} %copy.62.refs_5_, ...), custom_call_target="tpu_custom_call" | custom-call | flops 16000000000 | bytes 3674168 | tf_op jit(solution)/shard_map/pallas_call | solution.py:99
  125.2 3.5 %shard_map.168 = (bf16[256,2944]{1,0:T(8,128)(2,1)S(1)}, f32[256,2944]{1,0:T(8,128)S(1)}) custom-call(s32[2]{0:T(128)S(1)} %copy-done.28, bf16[4,512,128]{2,1,0:T(8,128)(2,1)S(1)} %copy-done.32, bf16[128,2880]{1,0:T(8,128)(2,1)S(1)} %copy-done.8, bf16[64,2944]{1,0:T(8,128)(2,1)S(1)} %copy-done.6, bf16[128,2944]{1,0:T(8,128)(2,1)} %get-tuple-element.89.rest_1_, ...), custom_call_target="tpu_custom_call" | custom-call | flops 4000000000 | bytes 3522568 | tf_op jit(solution)/shard_map/pallas_call | solution.py:99
  133.9 17.4 %collective-permute-done.22.got_ref = bf16[128,2944]{1,0:T(8,128)(2,1)S(1)} collective-permute-done((bf16[128,2944]{1,0:T(8,128)(2,1)S(1)}, bf16[128,2944]{1,0:T(8,128)(2,1)S(1)}, u32[]{:S(2)}, u32[]{:S(2)}) %collective-permute-start.22) | collective-permute-done | bytes 753696 | tf_op jit(solution)/shard_map/ppermute | solution.py:23
  151.9 8.2 %collective-permute-start.24 = (bf16[128,2944]{1,0:T(8,128)(2,1)S(1)}, bf16[128,2944]{1,0:T(8,128)(2,1)S(1)}, u32[]{:S(2)}, u32[]{:S(2)}) collective-permute-start(bf16[128,2944]{1,0:T(8,128)(2,1)S(1)} %get-tuple-element.96), channel_id=1, source_target_pairs={{0,8},{1,9},{2,10},{3,11},{4,12},{5,13},{6,14},{7,15},{8,0},{9,1},... | collective-permute-start | bytes 2261000 | tf_op jit(solution)/shard_map/ppermute | solution.py:23
  160.4 4.8 %collective-permute-start.23 = (bf16[128,2944]{1,0:T(8,128)(2,1)S(1)}, bf16[128,2944]{1,0:T(8,128)(2,1)S(1)}, u32[]{:S(2)}, u32[]{:S(2)}) collective-permute-start(bf16[128,2944]{1,0:T(8,128)(2,1)S(1)} %get-tuple-element.96), channel_id=1, source_target_pairs={{0,4},{1,5},{2,6},{3,7},{4,0},{5,1},{6,2},{7,3},{8,12},{9,13},{10,... | collective-permute-start | bytes 2261000 | tf_op jit(solution)/shard_map/ppermute | solution.py:23
  167.5 25.1 %collective-permute-done.24 = bf16[128,2944]{1,0:T(8,128)(2,1)S(1)} collective-permute-done((bf16[128,2944]{1,0:T(8,128)(2,1)S(1)}, bf16[128,2944]{1,0:T(8,128)(2,1)S(1)}, u32[]{:S(2)}, u32[]{:S(2)}) %collective-permute-start.24) | collective-permute-done | bytes 753696 | tf_op jit(solution)/shard_map/ppermute | solution.py:23
  197.0 13.3 %collective-permute-done.27 = bf16[128,2944]{1,0:T(8,128)(2,1)S(1)} collective-permute-done((bf16[128,2944]{1,0:T(8,128)(2,1)S(1)}, bf16[128,2944]{1,0:T(8,128)(2,1)S(1)}, u32[]{:S(2)}, u32[]{:S(2)}) %collective-permute-start.27) | collective-permute-done | bytes 753696 | tf_op jit(solution)/shard_map/ppermute | solution.py:23
  213.0 2.3 collective-permute-done.29
  215.4 7.8 %collective-permute-done.28 = bf16[72,2944]{1,0:T(8,128)(2,1)S(1)} collective-permute-done((bf16[72,2944]{1,0:T(8,128)(2,1)S(1)}, bf16[72,2944]{1,0:T(8,128)(2,1)S(1)}, u32[]{:S(2)}, u32[]{:S(2)}) %collective-permute-start.28) | collective-permute-done | bytes 423968 | tf_op jit(solution)/shard_map/ppermute | solution.py:23
  223.4 14.2 %shard_map.172 = bf16[288,2944]{1,0:T(8,128)(2,1)S(1)} custom-call(bf16[288,2944]{1,0:T(8,128)(2,1)S(1)} %pad_maximum_fusion.1.x_ref, f32[288,1]{1,0:T(8,128)S(1)} %broadcast_in_dim.80.row_ref, bf16[2,2880,768]{2,1,0:T(8,128)(2,1)} %all-gather.4.cloned.1.call-done.gate_ref, bf16[2,2880,768]{2,1,0:T(8,128)(2,1)} %all-gather.6.cloned.1.call-done.up_ref, ...), custom_call_target="tpu_custom_call" | custom-call | flops 7644119040 | bytes 26542080 | tf_op jit(solution)/shard_map/pallas_call | solution.py:646
  240.5 7.8 %collective-permute-done.31 = bf16[72,2944]{1,0:T(8,128)(2,1)S(1)} collective-permute-done((bf16[72,2944]{1,0:T(8,128)(2,1)S(1)}, bf16[72,2944]{1,0:T(8,128)(2,1)S(1)}, u32[]{:S(2)}, u32[]{:S(2)}) %collective-permute-start.31) | collective-permute-done | bytes 423968 | tf_op jit(solution)/shard_map/ppermute | solution.py:23
  249.9 14.4 %shard_map.171 = bf16[288,2944]{1,0:T(8,128)(2,1)S(1)} custom-call(bf16[288,2944]{1,0:T(8,128)(2,1)S(1)} %pad_maximum_fusion.x_ref, f32[288,1]{1,0:T(8,128)S(1)} %broadcast_in_dim.79.row_ref, bf16[2,2880,768]{2,1,0:T(8,128)(2,1)} %all-gather.4.cloned.1.call-done.gate_ref, bf16[2,2880,768]{2,1,0:T(8,128)(2,1)} %all-gather.6.cloned.1.call-done.up_ref, ...), custom_call_target="tpu_custom_call" | custom-call | flops 7644119040 | bytes 26542080 | tf_op jit(solution)/shard_map/pallas_call | solution.py:646
  265.4 2.1 collective-permute-done.32
  268.0 3.3 %collective-permute-start.35 = (bf16[128,2944]{1,0:T(8,128)(2,1)S(1)}, bf16[128,2944]{1,0:T(8,128)(2,1)S(1)}, u32[]{:S(2)}, u32[]{:S(2)}) collective-permute-start(bf16[128,2944]{1,0:T(8,128)(2,1)S(1)} %fusion.2), channel_id=1, source_target_pairs={{0,8},{1,9},{2,10},{3,11},{4,12},{5,13},{6,14},{7,15},{8,0},{9,1},... | collective-permute-start | bytes 2261000 | tf_op jit(solution)/shard_map/ppermute | solution.py:23
  275.0 6.6 %collective-permute-done.26 = bf16[72,2944]{1,0:T(8,128)(2,1)S(1)} collective-permute-done((bf16[72,2944]{1,0:T(8,128)(2,1)S(1)}, bf16[72,2944]{1,0:T(8,128)(2,1)S(1)}, u32[]{:S(2)}, u32[]{:S(2)}) %collective-permute-start.26) | collective-permute-done | bytes 423968 | tf_op jit(solution)/shard_map/ppermute | solution.py:23
  282.1 19.4 %collective-permute-done.35.rest_1_ = bf16[128,2944]{1,0:T(8,128)(2,1)S(1)} collective-permute-done((bf16[128,2944]{1,0:T(8,128)(2,1)S(1)}, bf16[128,2944]{1,0:T(8,128)(2,1)S(1)}, u32[]{:S(2)}, u32[]{:S(2)}) %collective-permute-start.35) | collective-permute-done | bytes 753696 | tf_op jit(solution)/shard_map/ppermute | solution.py:23
  (234 shorter events, 65.2 us)
Async XLA Ops:
  6.5 216.8 %all-gather.4.cloned.1.call-start = ((), (), s32[]{:S(2)}) async-start(), calls=%async_computation | async-start | bytes 13271040 | tf_op jit(solution)/shard_map/all_gather | solution.py:693
  7.3 216.0 %all-gather.6.cloned.1.call-start = ((), (), s32[]{:S(2)}) async-start(), calls=%async_computation.1 | async-start | bytes 13271040 | tf_op jit(solution)/shard_map/all_gather | solution.py:693
  8.1 215.3 %all-gather.8.cloned.1.call-start = ((), (), s32[]{:S(2)}) async-start(), calls=%async_computation.2 | async-start | bytes 13271040 | tf_op jit(solution)/shard_map/all_gather | solution.py:693
  25.2 29.3 %collective-permute-start.7 = (bf16[128,2944]{1,0:T(8,128)(2,1)}, bf16[128,2944]{1,0:T(8,128)(2,1)S(1)}, u32[]{:S(2)}, u32[]{:S(2)}) collective-permute-start(bf16[128,2944]{1,0:T(8,128)(2,1)} %get-tuple-element.61), channel_id=1, source_target_pairs={{0,2},{1,3},{2,0},{3,1},{4,6},{5,7},{6,4},{7,5},{8,10},{9,11},{10,... | collective-permute-start | bytes 2261000 | tf_op jit(solution)/shard_map/ppermute | solution.py:23
  26.8 27.6 %collective-permute-start.3 = (bf16[360,512]{1,0:T(8,128)(2,1)S(1)}, bf16[360,512]{1,0:T(8,128)(2,1)S(1)}, u32[]{:S(2)}, u32[]{:S(2)}) collective-permute-start(bf16[360,512]{1,0:T(8,128)(2,1)S(1)} %get-tuple-element.59.refs_0_), channel_id=1, source_target_pairs={{0,4},{1,5},{2,6},{3,7},{4,0},{5,1},{6,2},{7,3},{8,12},{9,13},{10,... | collective-permute-start | bytes 1105928 | tf_op jit(solution)/shard_map/ppermute | solution.py:23
  28.3 26.1 %collective-permute-start.4 = (bf16[360,512]{1,0:T(8,128)(2,1)S(1)}, bf16[360,512]{1,0:T(8,128)(2,1)S(1)}, u32[]{:S(2)}, u32[]{:S(2)}) collective-permute-start(bf16[360,512]{1,0:T(8,128)(2,1)S(1)} %get-tuple-element.59.refs_0_), channel_id=1, source_target_pairs={{0,8},{1,9},{2,10},{3,11},{4,12},{5,13},{6,14},{7,15},{8,0},{9,1},... | collective-permute-start | bytes 1105928 | tf_op jit(solution)/shard_map/ppermute | solution.py:23
  30.9 21.1 %collective-permute-start.5 = (bf16[128,640]{1,0:T(8,128)(2,1)S(1)}, bf16[128,640]{1,0:T(8,128)(2,1)S(1)}, u32[]{:S(2)}, u32[]{:S(2)}) collective-permute-start(bf16[128,640]{1,0:T(8,128)(2,1)S(1)} %get-tuple-element.60.refs_3_), channel_id=1, source_target_pairs={{0,4},{1,5},{2,6},{3,7},{4,0},{5,1},{6,2},{7,3},{8,12},{9,13},{10,... | collective-permute-start | bytes 491528 | tf_op jit(solution)/shard_map/ppermute | solution.py:23
  31.3 23.0 %collective-permute-start.6 = (bf16[128,640]{1,0:T(8,128)(2,1)S(1)}, bf16[128,640]{1,0:T(8,128)(2,1)S(1)}, u32[]{:S(2)}, u32[]{:S(2)}) collective-permute-start(bf16[128,640]{1,0:T(8,128)(2,1)S(1)} %get-tuple-element.60.refs_3_), channel_id=1, source_target_pairs={{0,8},{1,9},{2,10},{3,11},{4,12},{5,13},{6,14},{7,15},{8,0},{9,1},... | collective-permute-start | bytes 491528 | tf_op jit(solution)/shard_map/ppermute | solution.py:23
  58.2 20.1 %collective-permute-start.12 = (bf16[64,2944]{1,0:T(8,128)(2,1)}, bf16[64,2944]{1,0:T(8,128)(2,1)S(1)}, u32[]{:S(2)}, u32[]{:S(2)}) collective-permute-start(bf16[64,2944]{1,0:T(8,128)(2,1)} %shard_map.158.refs_11_), channel_id=1, source_target_pairs={{0,8},{1,9},{2,10},{3,11},{4,12},{5,13},{6,14},{7,15},{8,0},{9,1},... | collective-permute-start | bytes 1130504 | tf_op jit(solution)/shard_map/ppermute | solution.py:23
  58.5 19.8 %collective-permute-start.10 = (bf16[360,512]{1,0:T(8,128)(2,1)S(1)}, bf16[360,512]{1,0:T(8,128)(2,1)S(1)}, u32[]{:S(2)}, u32[]{:S(2)}) collective-permute-start(bf16[360,512]{1,0:T(8,128)(2,1)S(1)} %copy-done.38), channel_id=1, source_target_pairs={{0,16},{16,0},{1,17},{17,1},{2,18},{18,2},{3,19},{19,3},{4,20},{20... | collective-permute-start | bytes 1105928 | tf_op jit(solution)/shard_map/ppermute | solution.py:23
  60.0 18.3 %collective-permute-start.8 = (bf16[360,512]{1,0:T(8,128)(2,1)S(1)}, bf16[360,512]{1,0:T(8,128)(2,1)}, u32[]{:S(2)}, u32[]{:S(2)}) collective-permute-start(bf16[360,512]{1,0:T(8,128)(2,1)S(1)} %copy-done.38), channel_id=1, source_target_pairs={{0,4},{1,5},{2,6},{3,7},{4,0},{5,1},{6,2},{7,3},{8,12},{9,13},{10,... | collective-permute-start | bytes 1105928 | tf_op jit(solution)/shard_map/ppermute | solution.py:23
  62.7 15.6 %collective-permute-start.9 = (bf16[360,512]{1,0:T(8,128)(2,1)S(1)}, bf16[360,512]{1,0:T(8,128)(2,1)S(1)}, u32[]{:S(2)}, u32[]{:S(2)}) collective-permute-start(bf16[360,512]{1,0:T(8,128)(2,1)S(1)} %copy-done.36), channel_id=1, source_target_pairs={{0,16},{16,0},{1,17},{17,1},{2,18},{18,2},{3,19},{19,3},{4,20},{20... | collective-permute-start | bytes 1105928 | tf_op jit(solution)/shard_map/ppermute | solution.py:23
  63.2 15.1 %collective-permute-start.11 = (bf16[128,640]{1,0:T(8,128)(2,1)S(1)}, bf16[128,640]{1,0:T(8,128)(2,1)S(1)}, u32[]{:S(2)}, u32[]{:S(2)}) collective-permute-start(bf16[128,640]{1,0:T(8,128)(2,1)S(1)} %copy-done.14), channel_id=1, source_target_pairs={{0,4},{1,5},{2,6},{3,7},{4,0},{5,1},{6,2},{7,3},{8,12},{9,13},{10,... | collective-permute-start | bytes 491528 | tf_op jit(solution)/shard_map/ppermute | solution.py:23
  81.6 18.5 %collective-permute-start.16 = (bf16[128,2944]{1,0:T(8,128)(2,1)S(1)}, bf16[128,2944]{1,0:T(8,128)(2,1)}, u32[]{:S(2)}, u32[]{:S(2)}) collective-permute-start(bf16[128,2944]{1,0:T(8,128)(2,1)S(1)} %shard_map.164), channel_id=1, source_target_pairs={{0,4},{1,5},{2,6},{3,7},{4,0},{5,1},{6,2},{7,3},{8,12},{9,13},{10,... | collective-permute-start | bytes 2261000 | tf_op jit(solution)/shard_map/ppermute | solution.py:23
  83.4 16.1 %collective-permute-start.15 = (bf16[512,640]{1,0:T(8,128)(2,1)S(1)}, bf16[512,640]{1,0:T(8,128)(2,1)}, u32[]{:S(2)}, u32[]{:S(2)}) collective-permute-start(bf16[512,640]{1,0:T(8,128)(2,1)S(1)} %shard_map.163.refs_3_), channel_id=1, source_target_pairs={{0,2},{1,3},{2,0},{3,1},{4,6},{5,7},{6,4},{7,5},{8,10},{9,11},{10,... | collective-permute-start | bytes 1966088 | tf_op jit(solution)/shard_map/ppermute | solution.py:23
  84.2 11.8 %collective-permute-start.17 = (bf16[64,2944]{1,0:T(8,128)(2,1)S(1)}, bf16[64,2944]{1,0:T(8,128)(2,1)}, u32[]{:S(2)}, u32[]{:S(2)}) collective-permute-start(bf16[64,2944]{1,0:T(8,128)(2,1)S(1)} %copy-done.5), channel_id=1, source_target_pairs={{0,16},{16,0},{1,17},{17,1},{2,18},{18,2},{3,19},{19,3},{4,20},{20... | collective-permute-start | bytes 1130504 | tf_op jit(solution)/shard_map/ppermute | solution.py:23
  89.9 12.2 %collective-permute-start.14 = (bf16[360,512]{1,0:T(8,128)(2,1)}, bf16[360,512]{1,0:T(8,128)(2,1)S(1)}, u32[]{:S(2)}, u32[]{:S(2)}) collective-permute-start(bf16[360,512]{1,0:T(8,128)(2,1)} %shard_map.162.refs_10_), channel_id=1, source_target_pairs={{0,16},{16,0},{1,17},{17,1},{2,18},{18,2},{3,19},{19,3},{4,20},{20... | collective-permute-start | bytes 1105928 | tf_op jit(solution)/shard_map/ppermute | solution.py:23
  102.9 10.6 %collective-permute-start.18 = (bf16[512,640]{1,0:T(8,128)(2,1)}, bf16[512,640]{1,0:T(8,128)(2,1)S(1)}, u32[]{:S(2)}, u32[]{:S(2)}) collective-permute-start(bf16[512,640]{1,0:T(8,128)(2,1)} %get-tuple-element.86.refs_6_), channel_id=1, source_target_pairs={{0,1},{1,0},{2,3},{3,2},{4,5},{5,4},{6,7},{7,6},{8,9},{9,8},{10,11... | collective-permute-start | bytes 1966088 | tf_op jit(solution)/shard_map/ppermute | solution.py:23
  102.9 10.7 %collective-permute-start.19 = (bf16[512,640]{1,0:T(8,128)(2,1)}, bf16[512,640]{1,0:T(8,128)(2,1)S(1)}, u32[]{:S(2)}, u32[]{:S(2)}) collective-permute-start(bf16[512,640]{1,0:T(8,128)(2,1)} %get-tuple-element.87.refs_7_), channel_id=1, source_target_pairs={{0,1},{1,0},{2,3},{3,2},{4,5},{5,4},{6,7},{7,6},{8,9},{9,8},{10,11... | collective-permute-start | bytes 1966088 | tf_op jit(solution)/shard_map/ppermute | solution.py:23
  103.4 20.8 %collective-permute-start.20 = (bf16[128,2944]{1,0:T(8,128)(2,1)}, bf16[128,2944]{1,0:T(8,128)(2,1)S(1)}, u32[]{:S(2)}, u32[]{:S(2)}) collective-permute-start(bf16[128,2944]{1,0:T(8,128)(2,1)} %get-tuple-element.89.rest_1_), channel_id=1, source_target_pairs={{0,16},{16,0},{1,17},{17,1},{2,18},{18,2},{3,19},{19,3},{4,20},{20... | collective-permute-start | bytes 2261000 | tf_op jit(solution)/shard_map/ppermute | solution.py:23
  132.4 18.9 %collective-permute-start.22 = (bf16[128,2944]{1,0:T(8,128)(2,1)S(1)}, bf16[128,2944]{1,0:T(8,128)(2,1)S(1)}, u32[]{:S(2)}, u32[]{:S(2)}) collective-permute-start(bf16[128,2944]{1,0:T(8,128)(2,1)S(1)} %get-tuple-element.94), channel_id=1, source_target_pairs={{0,2},{1,3},{2,0},{3,1},{4,6},{5,7},{6,4},{7,5},{8,10},{9,11},{10,... | collective-permute-start | bytes 2261000 | tf_op jit(solution)/shard_map/ppermute | solution.py:23
  151.9 40.7 %collective-permute-start.24 = (bf16[128,2944]{1,0:T(8,128)(2,1)S(1)}, bf16[128,2944]{1,0:T(8,128)(2,1)S(1)}, u32[]{:S(2)}, u32[]{:S(2)}) collective-permute-start(bf16[128,2944]{1,0:T(8,128)(2,1)S(1)} %get-tuple-element.96), channel_id=1, source_target_pairs={{0,8},{1,9},{2,10},{3,11},{4,12},{5,13},{6,14},{7,15},{8,0},{9,1},... | collective-permute-start | bytes 2261000 | tf_op jit(solution)/shard_map/ppermute | solution.py:23
  160.4 34.3 %collective-permute-start.23 = (bf16[128,2944]{1,0:T(8,128)(2,1)S(1)}, bf16[128,2944]{1,0:T(8,128)(2,1)S(1)}, u32[]{:S(2)}, u32[]{:S(2)}) collective-permute-start(bf16[128,2944]{1,0:T(8,128)(2,1)S(1)} %get-tuple-element.96), channel_id=1, source_target_pairs={{0,4},{1,5},{2,6},{3,7},{4,0},{5,1},{6,2},{7,3},{8,12},{9,13},{10,... | collective-permute-start | bytes 2261000 | tf_op jit(solution)/shard_map/ppermute | solution.py:23
  166.2 72.7 %collective-permute-start.25 = (bf16[72,2944]{1,0:T(8,128)(2,1)}, bf16[72,2944]{1,0:T(8,128)(2,1)}, u32[]{:S(2)}, u32[]{:S(2)}) collective-permute-start(bf16[72,2944]{1,0:T(8,128)(2,1)} %convolution_convert_fusion.4), channel_id=1, source_target_pairs={{0,2},{1,3},{2,0},{3,1},{4,6},{5,7},{6,4},{7,5},{8,10},{9,11},{10,... | collective-permute-start | bytes 1271816 | tf_op jit(solution)/shard_map/ppermute | solution.py:23
  192.6 17.7 %collective-permute-start.27 = (bf16[128,2944]{1,0:T(8,128)(2,1)S(1)}, bf16[128,2944]{1,0:T(8,128)(2,1)S(1)}, u32[]{:S(2)}, u32[]{:S(2)}) collective-permute-start(bf16[128,2944]{1,0:T(8,128)(2,1)S(1)} %collective-permute-done.24), channel_id=1, source_target_pairs={{0,4},{1,5},{2,6},{3,7},{4,0},{5,1},{6,2},{7,3},{8,12},{9,13},{10,... | collective-permute-start | bytes 2261000 | tf_op jit(solution)/shard_map/ppermute | solution.py:23
  193.5 19.5 %collective-permute-start.30 = (bf16[72,2944]{1,0:T(8,128)(2,1)S(1)}, bf16[72,2944]{1,0:T(8,128)(2,1)S(1)}, u32[]{:S(2)}, u32[]{:S(2)}) collective-permute-start(bf16[72,2944]{1,0:T(8,128)(2,1)S(1)} %convolution_convert_fusion.2), channel_id=1, source_target_pairs={{0,2},{1,3},{2,0},{3,1},{4,6},{5,7},{6,4},{7,5},{8,10},{9,11},{10,... | collective-permute-start | bytes 1271816 | tf_op jit(solution)/shard_map/ppermute | solution.py:23
  195.0 20.4 %collective-permute-start.29 = (bf16[72,2944]{1,0:T(8,128)(2,1)S(1)}, bf16[72,2944]{1,0:T(8,128)(2,1)S(1)}, u32[]{:S(2)}, u32[]{:S(2)}) collective-permute-start(bf16[72,2944]{1,0:T(8,128)(2,1)S(1)} %convolution_convert_fusion.3), channel_id=1, source_target_pairs={{0,2},{1,3},{2,0},{3,1},{4,6},{5,7},{6,4},{7,5},{8,10},{9,11},{10,... | collective-permute-start | bytes 1271816 | tf_op jit(solution)/shard_map/ppermute | solution.py:23
  210.6 12.6 %collective-permute-start.28 = (bf16[72,2944]{1,0:T(8,128)(2,1)S(1)}, bf16[72,2944]{1,0:T(8,128)(2,1)S(1)}, u32[]{:S(2)}, u32[]{:S(2)}) collective-permute-start(bf16[72,2944]{1,0:T(8,128)(2,1)S(1)} %convolution_convert_fusion), channel_id=1, source_target_pairs={{0,2},{1,3},{2,0},{3,1},{4,6},{5,7},{6,4},{7,5},{8,10},{9,11},{10,... | collective-permute-start | bytes 1271816 | tf_op jit(solution)/shard_map/ppermute | solution.py:23
  248.7 16.8 %collective-permute-start.34 = (bf16[128,2944]{1,0:T(8,128)(2,1)S(1)}, bf16[128,2944]{1,0:T(8,128)(2,1)S(1)}, u32[]{:S(2)}, u32[]{:S(2)}) collective-permute-start(bf16[128,2944]{1,0:T(8,128)(2,1)S(1)} %fusion.3), channel_id=1, source_target_pairs={{0,4},{1,5},{2,6},{3,7},{4,0},{5,1},{6,2},{7,3},{8,12},{9,13},{10,... | collective-permute-start | bytes 2261000 | tf_op jit(solution)/shard_map/ppermute | solution.py:23
  248.8 18.8 %collective-permute-start.32 = (bf16[144,2944]{1,0:T(8,128)(2,1)S(1)}, bf16[144,2944]{1,0:T(8,128)(2,1)S(1)}, u32[]{:S(2)}, u32[]{:S(2)}) collective-permute-start(bf16[144,2944]{1,0:T(8,128)(2,1)S(1)} %concatenate.28), channel_id=1, source_target_pairs={{0,2},{1,3},{2,0},{3,1},{4,6},{5,7},{6,4},{7,5},{8,10},{9,11},{10,... | collective-permute-start | bytes 2543624 | tf_op jit(solution)/shard_map/ppermute | solution.py:23
  268.0 33.5 %collective-permute-start.35 = (bf16[128,2944]{1,0:T(8,128)(2,1)S(1)}, bf16[128,2944]{1,0:T(8,128)(2,1)S(1)}, u32[]{:S(2)}, u32[]{:S(2)}) collective-permute-start(bf16[128,2944]{1,0:T(8,128)(2,1)S(1)} %fusion.2), channel_id=1, source_target_pairs={{0,8},{1,9},{2,10},{3,11},{4,12},{5,13},{6,14},{7,15},{8,0},{9,1},... | collective-permute-start | bytes 2261000 | tf_op jit(solution)/shard_map/ppermute | solution.py:23
  271.7 30.7 %collective-permute-start.33 = (bf16[128,2944]{1,0:T(8,128)(2,1)S(1)}, bf16[128,2944]{1,0:T(8,128)(2,1)S(1)}, u32[]{:S(2)}, u32[]{:S(2)}) collective-permute-start(bf16[128,2944]{1,0:T(8,128)(2,1)S(1)} %fusion.1), channel_id=1, source_target_pairs={{0,4},{1,5},{2,6},{3,7},{4,0},{5,1},{6,2},{7,3},{8,12},{9,13},{10,... | collective-permute-start | bytes 2261000 | tf_op jit(solution)/shard_map/ppermute | solution.py:23
  (59 other events, 330.1 us)
Sparse Core Ops, SparseCore 0:
  8.9 23.8 all-gather.3
  34.4 22.3 all-gather.5
  84.1 22.4 all-gather.7

commit v2 on v1

--- a/solution.py
+++ b/solution.py
@@ -538,30 +538,31 @@
 
 
 def add_core(keep, got):
-    rows, width = keep.shape[0] // 2, keep.shape[1]
-
-    def body(keep_ref, got_ref, send_ref, rest_ref):
-        rest_ref[...] = keep_ref[:rows] + got_ref[:rows].astype(jnp.float32)
-        send_ref[...] = (keep_ref[rows:] + got_ref[rows:].astype(jnp.float32)).astype(jnp.bfloat16)
-
-    return whole_call(
-        body,
-        [
-            jax.ShapeDtypeStruct((rows, width), jnp.bfloat16),
-            jax.ShapeDtypeStruct((rows, width), jnp.float32),
-        ],
-        (keep, got),
-        scalars=0,
-    )
-
-
-def mix(tokens, keep, got, gain):
-    rows, padded = tokens.shape
+    rows, width = keep.shape[0] // 4, keep.shape[1]
+
+    def body(keep_ref, got_ref, send_a, send_b, rest_a, rest_b):
+        for i, (rest_ref, send_ref) in enumerate(((rest_a, send_a), (rest_b, send_b))):
+            at = slice(i * rows, (i + 1) * rows)
+            far = slice((2 + i) * rows, (3 + i) * rows)
+            rest_ref[...] = keep_ref[at, :] + got_ref[at, :].astype(jnp.float32)
+            send_ref[...] = (keep_ref[far, :] + got_ref[far, :].astype(jnp.float32)).astype(
+                jnp.bfloat16
+            )
+
+    send = jax.ShapeDtypeStruct((rows, width), jnp.bfloat16)
+    rest = jax.ShapeDtypeStruct((rows, width), jnp.float32)
+    return whole_call(body, [send, send, rest, rest], (keep, got), scalars=0)
+
+
+def mix(part, tokens, keep, got, gain):
+    rows, padded = keep.shape
     width = gain.shape[0]
 
     def body(tokens_ref, keep_ref, got_ref, gain_ref, mixed_ref, in_ref):
         mixed = (
-            tokens_ref[...].astype(jnp.float32) + keep_ref[...] + got_ref[...].astype(jnp.float32)
+            tokens_ref[part * rows:(part + 1) * rows, :].astype(jnp.float32)
+            + keep_ref[...]
+            + got_ref[...].astype(jnp.float32)
         ).astype(jnp.bfloat16)
         mixed_ref[...] = mixed
         values = mixed.astype(jnp.float32)
@@ -573,23 +574,27 @@
     return whole_call(body, [shape, shape], (tokens, keep, got, gain), scalars=0)
 
 
-def finish(width, mixed, total, *got):
-    rows = mixed.shape[0]
-
-    def body(mixed_ref, total_ref, *rest):
-        out_ref = rest[-1]
+def finish(width, parts):
+    rows = sum(part[0].shape[0] for part in parts)
+    operands = [x for part in parts for x in part]
+
+    def body(*refs):
+        out_ref = refs[-1]
         for start in range(0, width, 128):
             size = min(128, width - start)
-            lanes = slice(start, start + size)
-            value = mixed_ref[:, lanes].astype(jnp.float32) + total_ref[:, lanes]
-            for ref in rest[:-1]:
-                value += ref[:, lanes].astype(jnp.float32)
-            if size < 128:
-                value = jnp.concatenate([value, jnp.zeros((rows, 128 - size), jnp.float32)], axis=1)
-            out_ref[lanes, :] = value.T[:size].astype(jnp.bfloat16)
+            values, first = [], 0
+            for part in parts:
+                value = None
+                for ref in refs[first:first + len(part)]:
+                    term = ref[:, start:start + 128].astype(jnp.float32)
+                    value = term if value is None else value + term
+                values.append(value)
+                first += len(part)
+            value = jnp.concatenate(values, axis=0)
+            out_ref[start:start + size, :] = value.T[:size].astype(jnp.bfloat16)
 
     out = jax.ShapeDtypeStruct((width, rows), jnp.bfloat16)
-    return whole_call(body, out, (mixed, total, *got), scalars=0).T
+    return whole_call(body, out, operands, scalars=0).T
 
 
 def by_columns(hidden, down):
@@ -792,8 +797,13 @@
         (own_kv, y_kv, c_kv, cy_kv), planes, cols,
     )
     send, keep = project(info, attended, w_out, wo_got, wo_twin, wo_ks)
-    send, keep = add_core(keep, swap_with(send, "ctx", 1))
-    mixed, expert_in = mix(tokens, keep, swap_with(send, "ctx", 2), moe_gain)
+    *sends, keep_a, keep_b = add_core(keep, swap_with(send, "ctx", 1))
+    got_a = swap_with(sends[0], "ctx", 2)
+    mixed_a, in_a = mix(0, tokens, keep_a, got_a, moe_gain)
+    blocks_a = over_planes(in_a, planes)
+    got_b = swap_with(gate(sends[1], got_a), "ctx", 2)
+    mixed_b, in_b = mix(1, tokens, keep_b, got_b, moe_gain)
+    blocks_b = over_planes(in_b, planes)
 
     def rows_for(pick, k, block):
         return jnp.dot(pick[k], block, preferred_element_type=jnp.float32).astype(jnp.bfloat16)
@@ -804,8 +814,8 @@
 
     last = planes - 1
     near, far, ready = {}, {}, []
-    first_rows, far[0] = sent(0, expert_in)
-    blocks = over_planes(expert_in, planes)
+    blocks = {k: joined(blocks_a[k], blocks_b[k]) for k in range(planes)}
+    first_rows, far[0] = sent(0, blocks[0])
     for k in range(planes - 1):
         near[k] = rows_for(pick_own, k, blocks[k])
         if k:
@@ -855,7 +865,7 @@
                 else:
                     ends.append(arrived)
         bit *= 2
-    return finish(model_width, mixed, sums[0], *ends)
+    return finish(model_width, [[joined(mixed_a, mixed_b), sums[0], *ends]])
 
 
 def solution(mesh):

time: 311 us -> 307 us (0.987)
  waiting for transfers between devices: 154 us -> 137 us
  starting transfers between devices: 48.8 us -> 58.8 us
    ppermute x36 -> x40, waiting for transfers between devices: 152 us -> 136 us  [swap_with(): lax.ppermute(x, axis, [(i, i ^ bits) for i in range(lax.axis_size(axis))])]
    ppermute x36 -> x40, starting transfers between devices: 48.8 us -> 58.7 us  [swap_with(): lax.ppermute(x, axis, [(i, i ^ bits) for i in range(lax.axis_size(axis))])]
    unnamed x105 -> x113, local copies, waits for them, and re-layouts: 16.5 us -> 19.5 us
    pallas_call x12 -> x18, Pallas kernels: 21.8 us -> 22.5 us  [whole_call(): pl.pallas_call(body, out_shape=out_shapes, in_specs=[smem] * scalars + [v...]
  transfers between devices with their start and end apart: 39 -> 43, of which waited for: 21 -> 22; matrix products, arithmetic and copies ran while one was open for 6% -> 6% of each run, Pallas kernels for 19% -> 19%
where the time goes in v2:
time: 307 us; the launch traced here: 308 us
  waiting for transfers between devices  137 us (45%)
  Pallas kernels  60.2 us (20%)
  starting transfers between devices  58.8 us (19%)
  local copies, waits for them, and re-layouts  22.9 us (7%)
  between operations  13.9 us (5%)
  matrix products  8.22 us (3%)
  other arithmetic  6.35 us (2%)
    ppermute x40, waiting for transfers between devices, swap_with(): lax.ppermute(x, axis, [(i, i ^ bits) for i in range(lax.axis_size(axis))])  136 us
    ppermute x40, starting transfers between devices, swap_with(): lax.ppermute(x, axis, [(i, i ^ bits) for i in range(lax.axis_size(axis))])  58.7 us
    pallas_call x2, Pallas kernels, expert(): pl.pallas_call(body, out_shape=jax.ShapeDtypeStruct((rows, padded), jnp.b...  28.6 us
    pallas_call x18, Pallas kernels, whole_call(): pl.pallas_call(body, out_shape=out_shapes, in_specs=[smem] * scalars + [v...  22.5 us
    unnamed x113, local copies, waits for them, and re-layouts  19.5 us
    pallas_call x1, Pallas kernels, make_queries(): pl.pallas_call(body, out_shape=jax.ShapeDtypeStruct((kv_heads, 2 * rows,...  7.11 us
  transfers between devices with their start and end apart: 43, of which 22 were waited for; matrix products, arithmetic and copies ran while one was open for 6% of the time, Pallas kernels for 19%

profile of v2, /device:TPU:0, one launch (start us, length us, event | category | flops | bytes accessed | tf_op | source)
XLA Modules:
  0.0 307.6 jit_solution(8478367512495283821)
XLA Ops:
  10.3 2.5 collective-permute-start.1
  18.6 3.7 %collective-permute-done.2.p3 = bf16[180,512]{1,0:T(8,128)(2,1)S(1)} collective-permute-done((bf16[180,512]{1,0:T(8,128)(2,1)S(1)}, bf16[180,512]{1,0:T(8,128)(2,1)S(1)}, u32[]{:S(2)}, u32[]{:S(2)}) %collective-permute-start.2) | collective-permute-done | bytes 184352 | tf_op jit(solution)/shard_map/ppermute | solution.py:23
  27.7 2.6 collective-permute-start.4
  31.1 2.3 copy.61.weight_ref.own_ref
  33.3 18.0 %collective-permute-done.5.refs_4_ = bf16[128,640]{1,0:T(8,128)(2,1)S(1)} collective-permute-done((bf16[128,640]{1,0:T(8,128)(2,1)S(1)}, bf16[128,640]{1,0:T(8,128)(2,1)S(1)}, u32[]{:S(2)}, u32[]{:S(2)}) %collective-permute-start.5) | collective-permute-done | bytes 163872 | tf_op jit(solution)/shard_map/ppermute | solution.py:23
  51.3 2.4 collective-permute-done.6.refs_5_
  59.4 2.7 collective-permute-start.8
  62.6 15.0 %collective-permute-done.11.refs_9_ = bf16[128,640]{1,0:T(8,128)(2,1)S(1)} collective-permute-done((bf16[128,640]{1,0:T(8,128)(2,1)S(1)}, bf16[128,640]{1,0:T(8,128)(2,1)S(1)}, u32[]{:S(2)}, u32[]{:S(2)}) %collective-permute-start.11) | collective-permute-done | bytes 163872 | tf_op jit(solution)/shard_map/ppermute | solution.py:23
  87.1 2.4 shard_map.161.refs_1_
  97.4 3.5 %collective-permute-done.15.refs_4_ = bf16[512,640]{1,0:T(8,128)(2,1)} collective-permute-done((bf16[512,640]{1,0:T(8,128)(2,1)S(1)}, bf16[512,640]{1,0:T(8,128)(2,1)}, u32[]{:S(2)}, u32[]{:S(2)}) %collective-permute-start.15) | collective-permute-done | bytes 655392 | tf_op jit(solution)/shard_map/ppermute | solution.py:23
  107.8 7.1 %shard_map.166.refs_3_ = bf16[4,1024,128]{2,1,0:T(8,128)(2,1)} custom-call(s32[2]{0:T(128)} %copy-done.32, bf16[8,512,360]{2,1,0:T(8,128)(2,1)} %copy-done, f32[512,128]{1,0:T(8,128)} %copy-done.47, f32[512,128]{1,0:T(8,128)} %copy-done.46, bf16[360,512]{1,0:T(8,128)(2,1)} %get-tuple-element.74.refs_4_, bf16[360,512]{1,0:T(8,128)(2,1)} %copy-done.36, ...), custom_call_target="tpu_custom_call" | custom-call | flops 8000000000 | bytes 8000000 | tf_op jit(solution)/shard_map/pallas_call | solution.py:328
  115.8 8.9 %shard_map.167.att_ref = bf16[4,512,128]{2,1,0:T(8,128)(2,1)} custom-call(s32[2]{0:T(128)} %copy-done.32, s32[4]{0:T(128)} %slice.125.refs_1_, f32[8]{0:T(128)} %reshape.74.refs_2_, bf16[4,1024,128]{2,1,0:T(8,128)(2,1)} %shard_map.166.refs_3_, s32[512,1]{1,0:T(8,128)} %copy.62.refs_4_, s32[512,1]{1,0:T(8,128)} %copy.63.refs_5_, ...), custom_call_target="tpu_custom_call" | custom-call | flops 16000000000 | bytes 3674168 | tf_op jit(solution)/shard_map/pallas_call | solution.py:99
  125.8 3.5 %shard_map.168 = (bf16[256,2944]{1,0:T(8,128)(2,1)S(1)}, f32[256,2944]{1,0:T(8,128)S(1)}) custom-call(s32[2]{0:T(128)S(1)} %copy-done.33, bf16[4,512,128]{2,1,0:T(8,128)(2,1)S(1)} %copy-done.37, bf16[128,2880]{1,0:T(8,128)(2,1)S(1)} %copy-done.8, bf16[64,2944]{1,0:T(8,128)(2,1)S(1)} %copy-done.6, bf16[128,2944]{1,0:T(8,128)(2,1)} %get-tuple-element.93.rest_1_, ...), custom_call_target="tpu_custom_call" | custom-call | flops 4000000000 | bytes 3522568 | tf_op jit(solution)/shard_map/pallas_call | solution.py:99
  134.6 9.2 %collective-permute-done.22.got_ref.refs_1_ = bf16[64,2944]{1,0:T(8,128)(2,1)S(1)} collective-permute-done((bf16[64,2944]{1,0:T(8,128)(2,1)S(1)}, bf16[64,2944]{1,0:T(8,128)(2,1)S(1)}, u32[]{:S(2)}, u32[]{:S(2)}) %collective-permute-start.22) | collective-permute-done | bytes 376864 | tf_op jit(solution)/shard_map/ppermute | solution.py:23
  148.0 8.3 %collective-permute-start.26 = (bf16[64,2944]{1,0:T(8,128)(2,1)S(1)}, bf16[64,2944]{1,0:T(8,128)(2,1)S(1)}, u32[]{:S(2)}, u32[]{:S(2)}) collective-permute-start(bf16[64,2944]{1,0:T(8,128)(2,1)S(1)} %get-tuple-element.103.refs_0_), channel_id=1, source_target_pairs={{0,8},{1,9},{2,10},{3,11},{4,12},{5,13},{6,14},{7,15},{8,0},{9,1},... | collective-permute-start | bytes 1130504 | tf_op jit(solution)/shard_map/ppermute | solution.py:23
  156.3 4.5 %collective-permute-start.24 = (bf16[64,2944]{1,0:T(8,128)(2,1)S(1)}, bf16[64,2944]{1,0:T(8,128)(2,1)S(1)}, u32[]{:S(2)}, u32[]{:S(2)}) collective-permute-start(bf16[64,2944]{1,0:T(8,128)(2,1)S(1)} %get-tuple-element.103.refs_0_), channel_id=1, source_target_pairs={{0,4},{1,5},{2,6},{3,7},{4,0},{5,1},{6,2},{7,3},{8,12},{9,13},{10,... | collective-permute-start | bytes 1130504 | tf_op jit(solution)/shard_map/ppermute | solution.py:23
  161.2 2.4 collective-permute-start.27
  163.5 4.5 %collective-permute-start.25 = (bf16[64,2944]{1,0:T(8,128)(2,1)S(1)}, bf16[64,2944]{1,0:T(8,128)(2,1)S(1)}, u32[]{:S(2)}, u32[]{:S(2)}) collective-permute-start(bf16[64,2944]{1,0:T(8,128)(2,1)S(1)} %get-tuple-element.104.refs_1_), channel_id=1, source_target_pairs={{0,4},{1,5},{2,6},{3,7},{4,0},{5,1},{6,2},{7,3},{8,12},{9,13},{10,... | collective-permute-start | bytes 1130504 | tf_op jit(solution)/shard_map/ppermute | solution.py:23
  170.5 3.7 %collective-permute-done.26.refs_0_ = bf16[64,2944]{1,0:T(8,128)(2,1)S(1)} collective-permute-done((bf16[64,2944]{1,0:T(8,128)(2,1)S(1)}, bf16[64,2944]{1,0:T(8,128)(2,1)S(1)}, u32[]{:S(2)}, u32[]{:S(2)}) %collective-permute-start.26) | collective-permute-done | bytes 376864 | tf_op jit(solution)/shard_map/ppermute | solution.py:23
  175.0 13.7 %collective-permute-done.27.refs_1_ = bf16[64,2944]{1,0:T(8,128)(2,1)S(1)} collective-permute-done((bf16[64,2944]{1,0:T(8,128)(2,1)S(1)}, bf16[64,2944]{1,0:T(8,128)(2,1)S(1)}, u32[]{:S(2)}, u32[]{:S(2)}) %collective-permute-start.27) | collective-permute-done | bytes 376864 | tf_op jit(solution)/shard_map/ppermute | solution.py:23
  193.2 5.1 %collective-permute-done.30.refs_0_ = bf16[64,2944]{1,0:T(8,128)(2,1)S(1)} collective-permute-done((bf16[64,2944]{1,0:T(8,128)(2,1)S(1)}, bf16[64,2944]{1,0:T(8,128)(2,1)S(1)}, u32[]{:S(2)}, u32[]{:S(2)}) %collective-permute-start.30) | collective-permute-done | bytes 376864 | tf_op jit(solution)/shard_map/ppermute | solution.py:23
  198.3 6.5 %collective-permute-done.31.refs_1_ = bf16[64,2944]{1,0:T(8,128)(2,1)S(1)} collective-permute-done((bf16[64,2944]{1,0:T(8,128)(2,1)S(1)}, bf16[64,2944]{1,0:T(8,128)(2,1)S(1)}, u32[]{:S(2)}, u32[]{:S(2)}) %collective-permute-start.31) | collective-permute-done | bytes 376864 | tf_op jit(solution)/shard_map/ppermute | solution.py:23
  207.5 2.3 collective-permute-done.33
  209.8 7.4 %collective-permute-done.32 = bf16[72,2944]{1,0:T(8,128)(2,1)S(1)} collective-permute-done((bf16[72,2944]{1,0:T(8,128)(2,1)S(1)}, bf16[72,2944]{1,0:T(8,128)(2,1)S(1)}, u32[]{:S(2)}, u32[]{:S(2)}) %collective-permute-start.32) | collective-permute-done | bytes 423968 | tf_op jit(solution)/shard_map/ppermute | solution.py:23
  217.4 14.2 %shard_map.179 = bf16[288,2944]{1,0:T(8,128)(2,1)S(1)} custom-call(bf16[288,2944]{1,0:T(8,128)(2,1)S(1)} %pad_maximum_fusion.1.x_ref, f32[288,1]{1,0:T(8,128)S(1)} %broadcast_in_dim.81.row_ref, bf16[2,2880,768]{2,1,0:T(8,128)(2,1)} %all-gather.4.cloned.1.call-done.gate_ref, bf16[2,2880,768]{2,1,0:T(8,128)(2,1)} %all-gather.6.cloned.1.call-done.up_ref, ...), custom_call_target="tpu_custom_call" | custom-call | flops 7644119040 | bytes 26542080 | tf_op jit(solution)/shard_map/pallas_call | solution.py:651
  234.4 7.5 %collective-permute-done.35 = bf16[72,2944]{1,0:T(8,128)(2,1)S(1)} collective-permute-done((bf16[72,2944]{1,0:T(8,128)(2,1)S(1)}, bf16[72,2944]{1,0:T(8,128)(2,1)S(1)}, u32[]{:S(2)}, u32[]{:S(2)}) %collective-permute-start.35) | collective-permute-done | bytes 423968 | tf_op jit(solution)/shard_map/ppermute | solution.py:23
  242.2 3.2 %collective-permute-start.38 = (bf16[128,2944]{1,0:T(8,128)(2,1)S(1)}, bf16[128,2944]{1,0:T(8,128)(2,1)S(1)}, u32[]{:S(2)}, u32[]{:S(2)}) collective-permute-start(bf16[128,2944]{1,0:T(8,128)(2,1)S(1)} %fusion.3), channel_id=1, source_target_pairs={{0,4},{1,5},{2,6},{3,7},{4,0},{5,1},{6,2},{7,3},{8,12},{9,13},{10,... | collective-permute-start | bytes 2261000 | tf_op jit(solution)/shard_map/ppermute | solution.py:23
  246.4 14.4 %shard_map.177 = bf16[288,2944]{1,0:T(8,128)(2,1)S(1)} custom-call(bf16[288,2944]{1,0:T(8,128)(2,1)S(1)} %pad_maximum_fusion.x_ref, f32[288,1]{1,0:T(8,128)S(1)} %broadcast_in_dim.80.row_ref, bf16[2,2880,768]{2,1,0:T(8,128)(2,1)} %all-gather.4.cloned.1.call-done.gate_ref, bf16[2,2880,768]{2,1,0:T(8,128)(2,1)} %all-gather.6.cloned.1.call-done.up_ref, ...), custom_call_target="tpu_custom_call" | custom-call | flops 7644119040 | bytes 26542080 | tf_op jit(solution)/shard_map/pallas_call | solution.py:651
  261.6 2.5 collective-permute-done.36
  264.6 3.2 %collective-permute-start.39 = (bf16[128,2944]{1,0:T(8,128)(2,1)S(1)}, bf16[128,2944]{1,0:T(8,128)(2,1)S(1)}, u32[]{:S(2)}, u32[]{:S(2)}) collective-permute-start(bf16[128,2944]{1,0:T(8,128)(2,1)S(1)} %fusion.2), channel_id=1, source_target_pairs={{0,8},{1,9},{2,10},{3,11},{4,12},{5,13},{6,14},{7,15},{8,0},{9,1},... | collective-permute-start | bytes 2261000 | tf_op jit(solution)/shard_map/ppermute | solution.py:23
  270.3 6.9 %collective-permute-done.29 = bf16[72,2944]{1,0:T(8,128)(2,1)S(1)} collective-permute-done((bf16[72,2944]{1,0:T(8,128)(2,1)S(1)}, bf16[72,2944]{1,0:T(8,128)(2,1)S(1)}, u32[]{:S(2)}, u32[]{:S(2)}) %collective-permute-start.29) | collective-permute-done | bytes 423968 | tf_op jit(solution)/shard_map/ppermute | solution.py:23
  277.6 20.5 %collective-permute-done.39.refs_3_ = bf16[128,2944]{1,0:T(8,128)(2,1)S(1)} collective-permute-done((bf16[128,2944]{1,0:T(8,128)(2,1)S(1)}, bf16[128,2944]{1,0:T(8,128)(2,1)S(1)}, u32[]{:S(2)}, u32[]{:S(2)}) %collective-permute-start.39) | collective-permute-done | bytes 753696 | tf_op jit(solution)/shard_map/ppermute | solution.py:23
  (257 shorter events, 79.0 us)
Async XLA Ops:
  6.5 210.8 %all-gather.4.cloned.1.call-start = ((), (), s32[]{:S(2)}) async-start(), calls=%async_computation | async-start | bytes 13271040 | tf_op jit(solution)/shard_map/all_gather | solution.py:698
  7.3 210.0 %all-gather.6.cloned.1.call-start = ((), (), s32[]{:S(2)}) async-start(), calls=%async_computation.1 | async-start | bytes 13271040 | tf_op jit(solution)/shard_map/all_gather | solution.py:698
  8.1 209.3 %all-gather.8.cloned.1.call-start = ((), (), s32[]{:S(2)}) async-start(), calls=%async_computation.2 | async-start | bytes 13271040 | tf_op jit(solution)/shard_map/all_gather | solution.py:698
  24.6 29.2 %collective-permute-start.7 = (bf16[128,2944]{1,0:T(8,128)(2,1)}, bf16[128,2944]{1,0:T(8,128)(2,1)S(1)}, u32[]{:S(2)}, u32[]{:S(2)}) collective-permute-start(bf16[128,2944]{1,0:T(8,128)(2,1)} %get-tuple-element.65), channel_id=1, source_target_pairs={{0,2},{1,3},{2,0},{3,1},{4,6},{5,7},{6,4},{7,5},{8,10},{9,11},{10,... | collective-permute-start | bytes 2261000 | tf_op jit(solution)/shard_map/ppermute | solution.py:23
  26.1 27.6 %collective-permute-start.3 = (bf16[360,512]{1,0:T(8,128)(2,1)S(1)}, bf16[360,512]{1,0:T(8,128)(2,1)S(1)}, u32[]{:S(2)}, u32[]{:S(2)}) collective-permute-start(bf16[360,512]{1,0:T(8,128)(2,1)S(1)} %get-tuple-element.63.refs_0_), channel_id=1, source_target_pairs={{0,4},{1,5},{2,6},{3,7},{4,0},{5,1},{6,2},{7,3},{8,12},{9,13},{10,... | collective-permute-start | bytes 1105928 | tf_op jit(solution)/shard_map/ppermute | solution.py:23
  27.7 26.1 %collective-permute-start.4 = (bf16[360,512]{1,0:T(8,128)(2,1)S(1)}, bf16[360,512]{1,0:T(8,128)(2,1)S(1)}, u32[]{:S(2)}, u32[]{:S(2)}) collective-permute-start(bf16[360,512]{1,0:T(8,128)(2,1)S(1)} %get-tuple-element.63.refs_0_), channel_id=1, source_target_pairs={{0,8},{1,9},{2,10},{3,11},{4,12},{5,13},{6,14},{7,15},{8,0},{9,1},... | collective-permute-start | bytes 1105928 | tf_op jit(solution)/shard_map/ppermute | solution.py:23
  30.3 21.1 %collective-permute-start.5 = (bf16[128,640]{1,0:T(8,128)(2,1)S(1)}, bf16[128,640]{1,0:T(8,128)(2,1)S(1)}, u32[]{:S(2)}, u32[]{:S(2)}) collective-permute-start(bf16[128,640]{1,0:T(8,128)(2,1)S(1)} %get-tuple-element.64.refs_3_), channel_id=1, source_target_pairs={{0,4},{1,5},{2,6},{3,7},{4,0},{5,1},{6,2},{7,3},{8,12},{9,13},{10,... | collective-permute-start | bytes 491528 | tf_op jit(solution)/shard_map/ppermute | solution.py:23
  30.7 23.0 %collective-permute-start.6 = (bf16[128,640]{1,0:T(8,128)(2,1)S(1)}, bf16[128,640]{1,0:T(8,128)(2,1)S(1)}, u32[]{:S(2)}, u32[]{:S(2)}) collective-permute-start(bf16[128,640]{1,0:T(8,128)(2,1)S(1)} %get-tuple-element.64.refs_3_), channel_id=1, source_target_pairs={{0,8},{1,9},{2,10},{3,11},{4,12},{5,13},{6,14},{7,15},{8,0},{9,1},... | collective-permute-start | bytes 491528 | tf_op jit(solution)/shard_map/ppermute | solution.py:23
  57.5 20.1 %collective-permute-start.12 = (bf16[64,2944]{1,0:T(8,128)(2,1)}, bf16[64,2944]{1,0:T(8,128)(2,1)S(1)}, u32[]{:S(2)}, u32[]{:S(2)}) collective-permute-start(bf16[64,2944]{1,0:T(8,128)(2,1)} %shard_map.158.refs_11_), channel_id=1, source_target_pairs={{0,8},{1,9},{2,10},{3,11},{4,12},{5,13},{6,14},{7,15},{8,0},{9,1},... | collective-permute-start | bytes 1130504 | tf_op jit(solution)/shard_map/ppermute | solution.py:23
  57.9 19.7 %collective-permute-start.10 = (bf16[360,512]{1,0:T(8,128)(2,1)S(1)}, bf16[360,512]{1,0:T(8,128)(2,1)S(1)}, u32[]{:S(2)}, u32[]{:S(2)}) collective-permute-start(bf16[360,512]{1,0:T(8,128)(2,1)S(1)} %copy-done.42), channel_id=1, source_target_pairs={{0,16},{16,0},{1,17},{17,1},{2,18},{18,2},{3,19},{19,3},{4,20},{20... | collective-permute-start | bytes 1105928 | tf_op jit(solution)/shard_map/ppermute | solution.py:23
  59.4 18.2 %collective-permute-start.8 = (bf16[360,512]{1,0:T(8,128)(2,1)S(1)}, bf16[360,512]{1,0:T(8,128)(2,1)S(1)}, u32[]{:S(2)}, u32[]{:S(2)}) collective-permute-start(bf16[360,512]{1,0:T(8,128)(2,1)S(1)} %copy-done.42), channel_id=1, source_target_pairs={{0,4},{1,5},{2,6},{3,7},{4,0},{5,1},{6,2},{7,3},{8,12},{9,13},{10,... | collective-permute-start | bytes 1105928 | tf_op jit(solution)/shard_map/ppermute | solution.py:23
  62.1 15.6 %collective-permute-start.9 = (bf16[360,512]{1,0:T(8,128)(2,1)S(1)}, bf16[360,512]{1,0:T(8,128)(2,1)S(1)}, u32[]{:S(2)}, u32[]{:S(2)}) collective-permute-start(bf16[360,512]{1,0:T(8,128)(2,1)S(1)} %copy-done.40), channel_id=1, source_target_pairs={{0,16},{16,0},{1,17},{17,1},{2,18},{18,2},{3,19},{19,3},{4,20},{20... | collective-permute-start | bytes 1105928 | tf_op jit(solution)/shard_map/ppermute | solution.py:23
  62.6 15.0 %collective-permute-start.11 = (bf16[128,640]{1,0:T(8,128)(2,1)S(1)}, bf16[128,640]{1,0:T(8,128)(2,1)S(1)}, u32[]{:S(2)}, u32[]{:S(2)}) collective-permute-start(bf16[128,640]{1,0:T(8,128)(2,1)S(1)} %copy-done.18), channel_id=1, source_target_pairs={{0,4},{1,5},{2,6},{3,7},{4,0},{5,1},{6,2},{7,3},{8,12},{9,13},{10,... | collective-permute-start | bytes 491528 | tf_op jit(solution)/shard_map/ppermute | solution.py:23
  83.0 18.7 %collective-permute-start.16 = (bf16[128,2944]{1,0:T(8,128)(2,1)}, bf16[128,2944]{1,0:T(8,128)(2,1)}, u32[]{:S(2)}, u32[]{:S(2)}) collective-permute-start(bf16[128,2944]{1,0:T(8,128)(2,1)} %shard_map.164), channel_id=1, source_target_pairs={{0,4},{1,5},{2,6},{3,7},{4,0},{5,1},{6,2},{7,3},{8,12},{9,13},{10,... | collective-permute-start | bytes 2261000 | tf_op jit(solution)/shard_map/ppermute | solution.py:23
  84.7 16.1 %collective-permute-start.15 = (bf16[512,640]{1,0:T(8,128)(2,1)S(1)}, bf16[512,640]{1,0:T(8,128)(2,1)}, u32[]{:S(2)}, u32[]{:S(2)}) collective-permute-start(bf16[512,640]{1,0:T(8,128)(2,1)S(1)} %shard_map.163.refs_3_), channel_id=1, source_target_pairs={{0,2},{1,3},{2,0},{3,1},{4,6},{5,7},{6,4},{7,5},{8,10},{9,11},{10,... | collective-permute-start | bytes 1966088 | tf_op jit(solution)/shard_map/ppermute | solution.py:23
  91.3 12.2 %collective-permute-start.14 = (bf16[360,512]{1,0:T(8,128)(2,1)}, bf16[360,512]{1,0:T(8,128)(2,1)S(1)}, u32[]{:S(2)}, u32[]{:S(2)}) collective-permute-start(bf16[360,512]{1,0:T(8,128)(2,1)} %shard_map.162.refs_10_), channel_id=1, source_target_pairs={{0,16},{16,0},{1,17},{17,1},{2,18},{18,2},{3,19},{19,3},{4,20},{20... | collective-permute-start | bytes 1105928 | tf_op jit(solution)/shard_map/ppermute | solution.py:23
  104.8 20.0 %collective-permute-start.20 = (bf16[128,2944]{1,0:T(8,128)(2,1)}, bf16[128,2944]{1,0:T(8,128)(2,1)S(1)}, u32[]{:S(2)}, u32[]{:S(2)}) collective-permute-start(bf16[128,2944]{1,0:T(8,128)(2,1)} %get-tuple-element.93.rest_1_), channel_id=1, source_target_pairs={{0,16},{16,0},{1,17},{17,1},{2,18},{18,2},{3,19},{19,3},{4,20},{20... | collective-permute-start | bytes 2261000 | tf_op jit(solution)/shard_map/ppermute | solution.py:23
  144.6 16.2 %collective-permute-start.23 = (bf16[64,2944]{1,0:T(8,128)(2,1)}, bf16[64,2944]{1,0:T(8,128)(2,1)S(1)}, u32[]{:S(2)}, u32[]{:S(2)}) collective-permute-start(bf16[64,2944]{1,0:T(8,128)(2,1)} %shard_map.171), channel_id=1, source_target_pairs={{0,2},{1,3},{2,0},{3,1},{4,6},{5,7},{6,4},{7,5},{8,10},{9,11},{10,... | collective-permute-start | bytes 1130504 | tf_op jit(solution)/shard_map/ppermute | solution.py:23
  148.0 26.2 %collective-permute-start.26 = (bf16[64,2944]{1,0:T(8,128)(2,1)S(1)}, bf16[64,2944]{1,0:T(8,128)(2,1)S(1)}, u32[]{:S(2)}, u32[]{:S(2)}) collective-permute-start(bf16[64,2944]{1,0:T(8,128)(2,1)S(1)} %get-tuple-element.103.refs_0_), channel_id=1, source_target_pairs={{0,8},{1,9},{2,10},{3,11},{4,12},{5,13},{6,14},{7,15},{8,0},{9,1},... | collective-permute-start | bytes 1130504 | tf_op jit(solution)/shard_map/ppermute | solution.py:23
  156.3 33.7 %collective-permute-start.24 = (bf16[64,2944]{1,0:T(8,128)(2,1)S(1)}, bf16[64,2944]{1,0:T(8,128)(2,1)S(1)}, u32[]{:S(2)}, u32[]{:S(2)}) collective-permute-start(bf16[64,2944]{1,0:T(8,128)(2,1)S(1)} %get-tuple-element.103.refs_0_), channel_id=1, source_target_pairs={{0,4},{1,5},{2,6},{3,7},{4,0},{5,1},{6,2},{7,3},{8,12},{9,13},{10,... | collective-permute-start | bytes 1130504 | tf_op jit(solution)/shard_map/ppermute | solution.py:23
  161.2 27.5 %collective-permute-start.27 = (bf16[64,2944]{1,0:T(8,128)(2,1)S(1)}, bf16[64,2944]{1,0:T(8,128)(2,1)S(1)}, u32[]{:S(2)}, u32[]{:S(2)}) collective-permute-start(bf16[64,2944]{1,0:T(8,128)(2,1)S(1)} %get-tuple-element.104.refs_1_), channel_id=1, source_target_pairs={{0,8},{1,9},{2,10},{3,11},{4,12},{5,13},{6,14},{7,15},{8,0},{9,1},... | collective-permute-start | bytes 1130504 | tf_op jit(solution)/shard_map/ppermute | solution.py:23
  163.5 27.1 %collective-permute-start.25 = (bf16[64,2944]{1,0:T(8,128)(2,1)S(1)}, bf16[64,2944]{1,0:T(8,128)(2,1)S(1)}, u32[]{:S(2)}, u32[]{:S(2)}) collective-permute-start(bf16[64,2944]{1,0:T(8,128)(2,1)S(1)} %get-tuple-element.104.refs_1_), channel_id=1, source_target_pairs={{0,4},{1,5},{2,6},{3,7},{4,0},{5,1},{6,2},{7,3},{8,12},{9,13},{10,... | collective-permute-start | bytes 1130504 | tf_op jit(solution)/shard_map/ppermute | solution.py:23
  169.4 63.2 %collective-permute-start.28 = (bf16[72,2944]{1,0:T(8,128)(2,1)}, bf16[72,2944]{1,0:T(8,128)(2,1)}, u32[]{:S(2)}, u32[]{:S(2)}) collective-permute-start(bf16[72,2944]{1,0:T(8,128)(2,1)} %convolution_convert_fusion.4), channel_id=1, source_target_pairs={{0,2},{1,3},{2,0},{3,1},{4,6},{5,7},{6,4},{7,5},{8,10},{9,11},{10,... | collective-permute-start | bytes 1271816 | tf_op jit(solution)/shard_map/ppermute | solution.py:23
  174.2 24.2 %collective-permute-start.30 = (bf16[64,2944]{1,0:T(8,128)(2,1)S(1)}, bf16[64,2944]{1,0:T(8,128)(2,1)S(1)}, u32[]{:S(2)}, u32[]{:S(2)}) collective-permute-start(bf16[64,2944]{1,0:T(8,128)(2,1)S(1)} %collective-permute-done.26.refs_0_), channel_id=1, source_target_pairs={{0,4},{1,5},{2,6},{3,7},{4,0},{5,1},{6,2},{7,3},{8,12},{9,13},{10,... | collective-permute-start | bytes 1130504 | tf_op jit(solution)/shard_map/ppermute | solution.py:23
  189.0 18.5 %collective-permute-start.34 = (bf16[72,2944]{1,0:T(8,128)(2,1)S(1)}, bf16[72,2944]{1,0:T(8,128)(2,1)S(1)}, u32[]{:S(2)}, u32[]{:S(2)}) collective-permute-start(bf16[72,2944]{1,0:T(8,128)(2,1)S(1)} %convolution_convert_fusion.2), channel_id=1, source_target_pairs={{0,2},{1,3},{2,0},{3,1},{4,6},{5,7},{6,4},{7,5},{8,10},{9,11},{10,... | collective-permute-start | bytes 1271816 | tf_op jit(solution)/shard_map/ppermute | solution.py:23
  190.0 14.8 %collective-permute-start.31 = (bf16[64,2944]{1,0:T(8,128)(2,1)S(1)}, bf16[64,2944]{1,0:T(8,128)(2,1)S(1)}, u32[]{:S(2)}, u32[]{:S(2)}) collective-permute-start(bf16[64,2944]{1,0:T(8,128)(2,1)S(1)} %collective-permute-done.27.refs_1_), channel_id=1, source_target_pairs={{0,4},{1,5},{2,6},{3,7},{4,0},{5,1},{6,2},{7,3},{8,12},{9,13},{10,... | collective-permute-start | bytes 1130504 | tf_op jit(solution)/shard_map/ppermute | solution.py:23
  191.0 18.8 %collective-permute-start.33 = (bf16[72,2944]{1,0:T(8,128)(2,1)S(1)}, bf16[72,2944]{1,0:T(8,128)(2,1)S(1)}, u32[]{:S(2)}, u32[]{:S(2)}) collective-permute-start(bf16[72,2944]{1,0:T(8,128)(2,1)S(1)} %convolution_convert_fusion.3), channel_id=1, source_target_pairs={{0,2},{1,3},{2,0},{3,1},{4,6},{5,7},{6,4},{7,5},{8,10},{9,11},{10,... | collective-permute-start | bytes 1271816 | tf_op jit(solution)/shard_map/ppermute | solution.py:23
  205.2 12.0 %collective-permute-start.32 = (bf16[72,2944]{1,0:T(8,128)(2,1)S(1)}, bf16[72,2944]{1,0:T(8,128)(2,1)S(1)}, u32[]{:S(2)}, u32[]{:S(2)}) collective-permute-start(bf16[72,2944]{1,0:T(8,128)(2,1)S(1)} %convolution_convert_fusion), channel_id=1, source_target_pairs={{0,2},{1,3},{2,0},{3,1},{4,6},{5,7},{6,4},{7,5},{8,10},{9,11},{10,... | collective-permute-start | bytes 1271816 | tf_op jit(solution)/shard_map/ppermute | solution.py:23
  242.2 19.4 %collective-permute-start.38 = (bf16[128,2944]{1,0:T(8,128)(2,1)S(1)}, bf16[128,2944]{1,0:T(8,128)(2,1)S(1)}, u32[]{:S(2)}, u32[]{:S(2)}) collective-permute-start(bf16[128,2944]{1,0:T(8,128)(2,1)S(1)} %fusion.3), channel_id=1, source_target_pairs={{0,4},{1,5},{2,6},{3,7},{4,0},{5,1},{6,2},{7,3},{8,12},{9,13},{10,... | collective-permute-start | bytes 2261000 | tf_op jit(solution)/shard_map/ppermute | solution.py:23
  245.4 18.7 %collective-permute-start.36 = (bf16[144,2944]{1,0:T(8,128)(2,1)S(1)}, bf16[144,2944]{1,0:T(8,128)(2,1)S(1)}, u32[]{:S(2)}, u32[]{:S(2)}) collective-permute-start(bf16[144,2944]{1,0:T(8,128)(2,1)S(1)} %concatenate.28), channel_id=1, source_target_pairs={{0,2},{1,3},{2,0},{3,1},{4,6},{5,7},{6,4},{7,5},{8,10},{9,11},{10,... | collective-permute-start | bytes 2543624 | tf_op jit(solution)/shard_map/ppermute | solution.py:23
  264.6 33.5 %collective-permute-start.39 = (bf16[128,2944]{1,0:T(8,128)(2,1)S(1)}, bf16[128,2944]{1,0:T(8,128)(2,1)S(1)}, u32[]{:S(2)}, u32[]{:S(2)}) collective-permute-start(bf16[128,2944]{1,0:T(8,128)(2,1)S(1)} %fusion.2), channel_id=1, source_target_pairs={{0,8},{1,9},{2,10},{3,11},{4,12},{5,13},{6,14},{7,15},{8,0},{9,1},... | collective-permute-start | bytes 2261000 | tf_op jit(solution)/shard_map/ppermute | solution.py:23
  268.3 31.5 %collective-permute-start.37 = (bf16[128,2944]{1,0:T(8,128)(2,1)S(1)}, bf16[128,2944]{1,0:T(8,128)(2,1)S(1)}, u32[]{:S(2)}, u32[]{:S(2)}) collective-permute-start(bf16[128,2944]{1,0:T(8,128)(2,1)S(1)} %fusion.1), channel_id=1, source_target_pairs={{0,4},{1,5},{2,6},{3,7},{4,0},{5,1},{6,2},{7,3},{8,12},{9,13},{10,... | collective-permute-start | bytes 2261000 | tf_op jit(solution)/shard_map/ppermute | solution.py:23
  (67 other events, 361.0 us)
Sparse Core Ops, SparseCore 0:
  8.9 23.8 all-gather.3
  34.4 22.3 all-gather.5
  85.6 22.9 all-gather.7
